TPU v7x, 32 devices: a whole 2x2x4 slice. The times are simulated.
32 devices in a mesh: gx: 4 (over x, core), gy: 8 (over z, y).
Axes of the slice: x: 2, y: 2, z: 4, core: 2. Of those that a mesh axis runs over, the one named last changes fastest.
Arguments:
- fine_atmospheric_values: float32 [4, 768, 768], P(None, 'gx', 'gy'), may hold values from -6 to 6
- fine_skin_heat: float32 [768, 768], P('gx', 'gy'), may hold values from -6 to 6
- coarse_lowest_values: bfloat16 [4, 1536, 3072], P(None, 'gx', 'gy'), may hold values from -6 to 6
- holder_flat: int32 [1], replicated, may hold values from 0 to 31
- corner_offset: int32 [2], replicated, may hold values from 0 to 264
- exchange_patch_holder: int32 [4608, 1], P(('gx', 'gy')), may hold values from 0 to 31; in each aligned block of 144 rows (0 to 143, 144 to 287, ...) at most 9 rows name the same one
- holder_patch_position: int32 [4608], P(('gx', 'gy')), may hold values from 0 to 31
- coarse_interface_exchange: float32 [4, 131072], P(None, ('gx', 'gy')), may hold values from -6 to 6
- marine_stratum_values: float32 [4, 41, 131072], P(None, None, ('gx', 'gy')), may hold values from -6 to 6
- diffusion_solver_operator: float32 [41, 41], replicated, may hold values from -0.3 to 1
Outputs:
- nest_next: float32 [4, 768, 768], P(None, 'gx', 'gy')
- refreshed_marine_values: float32 [4, 41, 131072], P(None, None, ('gx', 'gy'))
- fine_refreshed_skin_heat: float32 [768, 768], P('gx', 'gy')
Inputs may be any that keep to these rules, and one draw needn't show every extreme that they name: `holder_flat`: index of the tile that holds the storm. `corner_offset`: the nest lies inside the owner tile. `exchange_patch_holder`: within the blocks of one device, no ocean owner is named more than 9 times.
All inputs are finite; a program needn't handle non-finite values.
Results may differ from a plain program's by a relative error of at most 0.0019.
Values may be sent and summed in bfloat16 or wider, within the bound.
A program may use at most 64 MiB of HBM per device.

v0:
```python
import jax
import jax.numpy as jnp
from jax import lax
from jax.sharding import PartitionSpec as P

FIELDS = 4
EXCHANGE_PATCH = 128
MARINE_PATCHES = 32
STEPS = 4


diffuse_coef = 0.24
relax_coef = 0.3
drag_coefficient = 0.5


def spread(value, axis, root):
    mine = lax.axis_index(axis) == root
    return lax.psum(jnp.where(mine, value, jnp.zeros_like(value)), axis)


def extended(value, sides, width):
    for axis, dim in sides:
        devices, length = (lax.axis_size(axis), value.shape[dim])
        up = [(i, (i + 1) % devices) for i in range(devices - 1)]
        down = [(j, i) for i, j in up]
        last = lax.slice_in_dim(value, length - width, length, axis=dim)
        initial = lax.slice_in_dim(value, 0, width, axis=dim)
        before = lax.ppermute(last, axis, up)
        after = lax.ppermute(initial, axis, down)
        value = jnp.concatenate([before, value, after], axis=dim)
    return value


def hat_weights(cell_count, first_cell, anchor_cell, parent_cells):
    fine_cells = (jnp.arange(cell_count) + first_cell).astype(jnp.float32)
    centre = (fine_cells + 0.5) * (2.0 / 13.0) - 0.5 + anchor_cell.astype(jnp.float32)
    coarse = jnp.arange(parent_cells).astype(jnp.float32)
    return jnp.maximum(0.0, 1.0 - jnp.abs(centre[:, None] - coarse[None, :])).astype(jnp.bfloat16)


def interpolate(parent_part, corner_offset, first_x, count_x, first_y, count_y):
    weight_x = hat_weights(count_x, first_x, corner_offset[0], parent_part.shape[1])
    weight_y = hat_weights(count_y, first_y, corner_offset[1], parent_part.shape[2])
    partial_value = jnp.einsum(
        "fpq,jq->fpj", parent_part, weight_y, preferred_element_type=jnp.float32
    ).astype(jnp.bfloat16)
    return jnp.einsum("ip,fpj->fij", weight_x, partial_value, preferred_element_type=jnp.float32)


def on_device(
    fine_atmospheric_values,
    fine_skin_heat,
    coarse_lowest_values,
    holder_flat,
    corner_offset,
    exchange_patch_holder,
    holder_patch_position,
    coarse_interface_exchange,
    marine_stratum_values,
    diffusion_solver_operator,
):
    size_x = lax.axis_size("gx")
    size_y = lax.axis_size("gy")
    devices = size_x * size_y
    index_x = lax.axis_index("gx")
    index_y = lax.axis_index("gy")
    tile_column_index = fine_atmospheric_values.shape[1]
    tile_row_index = fine_atmospheric_values.shape[2]
    received = spread(coarse_lowest_values, ("gx", "gy"), holder_flat[0])
    start_x = index_x * tile_column_index
    start_y = index_y * tile_row_index
    forcing = interpolate(
        received, corner_offset, start_x, tile_column_index, start_y, tile_row_index
    )
    present_fine_values = fine_atmospheric_values
    for iteration in range(STEPS):
        padded = extended(present_fine_values, (("gx", 1), ("gy", 2)), 1)
        beside = (
            padded[:, 2:, 1:-1] + padded[:, :-2, 1:-1] + padded[:, 1:-1, 2:] + padded[:, 1:-1, :-2]
        )
        present_fine_values = (
            present_fine_values
            + diffuse_coef * (beside - 4.0 * present_fine_values)
            + relax_coef * (forcing - present_fine_values)
        )
    breeze_speed = jnp.sqrt(
        1.0
        + present_fine_values[0] * present_fine_values[0]
        + present_fine_values[1] * present_fine_values[1]
    )
    interface_exchange = jnp.stack(
        [
            drag_coefficient * breeze_speed * (present_fine_values[2] - fine_skin_heat),
            drag_coefficient * breeze_speed * (present_fine_values[3] - 0.5 * fine_skin_heat),
            drag_coefficient * breeze_speed * present_fine_values[0],
            drag_coefficient * breeze_speed * present_fine_values[1],
        ]
    )
    block_count = tile_column_index * tile_row_index // EXCHANGE_PATCH
    capacity = max(2, (2 * block_count + devices - 1) // devices)
    owner_list = exchange_patch_holder[:, 0]
    owners_hot = (owner_list[:, None] == jnp.arange(devices, dtype=jnp.int32)[None, :]).astype(
        jnp.int32
    )
    earlier = jnp.cumsum(owners_hot, axis=0) - owners_hot
    ranking = jnp.sum(earlier * owners_hot, axis=1)
    fine_grid_position = owner_list * capacity + ranking
    flux_rows = interface_exchange.reshape(FIELDS, block_count, EXCHANGE_PATCH)
    send_flux = (
        jnp.zeros((FIELDS, devices * capacity, EXCHANGE_PATCH), jnp.float32)
        .at[:, fine_grid_position]
        .set(flux_rows)
    )
    send_slot = (
        jnp.full((devices * capacity,), -1, jnp.int32)
        .at[fine_grid_position]
        .set(holder_patch_position)
    )
    got_flux, got_slot = (
        lax.all_to_all(
            send_flux.reshape(FIELDS, devices, capacity * EXCHANGE_PATCH),
            ("gx", "gy"),
            split_axis=1,
            concat_axis=1,
            tiled=True,
        ),
        lax.all_to_all(
            send_slot.reshape(1, devices, capacity),
            ("gx", "gy"),
            split_axis=1,
            concat_axis=1,
            tiled=True,
        ),
    )
    got_flux = got_flux.reshape(FIELDS, devices * capacity, EXCHANGE_PATCH)
    got_slot = got_slot.reshape(devices * capacity)
    patch_selector_hot = (
        got_slot[:, None] == jnp.arange(MARINE_PATCHES, dtype=jnp.int32)[None, :]
    ).astype(jnp.float32)
    block_sums = jnp.einsum(
        "ro,frc->foc", patch_selector_hot, got_flux, precision=lax.Precision.HIGHEST
    )
    counts = jnp.sum(patch_selector_hot, axis=0)
    coarse = coarse_interface_exchange.reshape(FIELDS, MARINE_PATCHES, EXCHANGE_PATCH)
    uncovered = (counts == 0.0).astype(jnp.float32)
    forcing_ocean = (block_sums + coarse * uncovered[None, :, None]) / jnp.maximum(counts, 1.0)[
        None, :, None
    ]
    forced = marine_stratum_values.at[:, 0, :].set(
        marine_stratum_values[:, 0, :]
        + forcing_ocean.reshape(FIELDS, MARINE_PATCHES * EXCHANGE_PATCH)
    )
    refreshed_marine_values = jnp.einsum(
        "lk,fkc->flc", diffusion_solver_operator, forced, precision=lax.Precision.HIGHEST
    )
    skin_heat_gather = refreshed_marine_values[0, 0].reshape(MARINE_PATCHES, EXCHANGE_PATCH)
    returned_patches = jnp.dot(
        patch_selector_hot, skin_heat_gather, precision=lax.Precision.HIGHEST
    )
    arrived_patches = lax.all_to_all(
        returned_patches.reshape(devices, capacity * EXCHANGE_PATCH),
        ("gx", "gy"),
        split_axis=0,
        concat_axis=0,
        tiled=True,
    )
    arrived_patches = arrived_patches.reshape(devices * capacity, EXCHANGE_PATCH)
    fine_refreshed_skin_heat = arrived_patches[fine_grid_position].reshape(
        tile_column_index, tile_row_index
    )
    return (present_fine_values, refreshed_marine_values, fine_refreshed_skin_heat)


def solution(mesh):
    in_specs = (
        P(None, "gx", "gy"),
        P("gx", "gy"),
        P(None, "gx", "gy"),
        P(),
        P(),
        P(("gx", "gy"), None),
        P(("gx", "gy")),
        P(None, ("gx", "gy")),
        P(None, None, ("gx", "gy")),
        P(),
    )
    out_specs = (P(None, "gx", "gy"), P(None, None, ("gx", "gy")), P("gx", "gy"))
    return jax.shard_map(
        on_device, mesh=mesh, in_specs=in_specs, out_specs=out_specs, check_vma=False
    )
```

profile of v0, /device:TPU:0, one launch (start us, length us, event | category | flops | bytes accessed | tf_op | source)
XLA Modules:
  0.0 282.2 jit_solution(6178498991566446043)
XLA Ops:
  9.8 1.3 collective-permute-start
  11.2 3.0 %collective-permute-start.1 = (f32[4,1,96]{1,2,0:T(8,128)S(1)}, f32[4,1,96]{1,2,0:T(8,128)S(1)}, u32[]{:S(2)}, u32[]{:S(2)}) collective-permute-start(f32[4,1,96]{1,2,0:T(8,128)S(1)} %copy.49), channel_id=1, source_target_pairs={{0,8},{8,16},{16,24},{1,9},{9,17},{17,25},{2,10},{10,18},{18,26},{... | collective-permute-start | bytes 4616 | tf_op jit(solution)/shard_map/ppermute | solution.py:29
  17.8 5.5 %collective-permute-start.3 = (f32[4,194,1]{1,2,0:T(1,128)S(1)}, f32[4,194,1]{1,2,0:T(1,128)S(1)}, u32[]{:S(2)}, u32[]{:S(2)}) collective-permute-start(f32[4,194,1]{1,2,0:T(1,128)S(1)} %get-tuple-element.33), channel_id=1, source_target_pairs={{0,1},{1,2},{2,3},{3,4},{4,5},{5,6},{6,7},{8,9},{9,10},{10,11},{11... | collective-permute-start | bytes 9320 | tf_op jit(solution)/shard_map/ppermute | solution.py:29
  24.6 123.1 %all-reduce.3.cloned.1.call-done = bf16[4,384,384]{2,1,0:T(8,128)(2,1)} async-done(((bf16[4,384,384]{2,1,0:T(8,128)(2,1)}), bf16[4,384,384]{2,1,0:T(8,128)(2,1)}) %all-reduce.3.cloned.1.call-update) | async-done | bytes 1179664 | tf_op jit(solution)/shard_map/psum | solution.py:19
  147.8 2.1 fusion.28
  151.2 3.0 %collective-permute-start.5 = (f32[4,1,96]{1,2,0:T(8,128)S(1)}, f32[4,1,96]{1,2,0:T(8,128)S(1)}, u32[]{:S(2)}, u32[]{:S(2)}) collective-permute-start(f32[4,1,96]{1,2,0:T(8,128)S(1)} %get-tuple-element.40), channel_id=1, source_target_pairs={{0,8},{8,16},{16,24},{1,9},{9,17},{17,25},{2,10},{10,18},{18,26},{... | collective-permute-start | bytes 4616 | tf_op jit(solution)/shard_map/ppermute | solution.py:29
  156.7 4.5 %collective-permute-start.7 = (f32[4,194,1]{1,2,0:T(1,128)S(1)}, f32[4,194,1]{1,2,0:T(1,128)S(1)}, u32[]{:S(2)}, u32[]{:S(2)}) collective-permute-start(f32[4,194,1]{1,2,0:T(1,128)S(1)} %get-tuple-element.31), channel_id=1, source_target_pairs={{0,1},{1,2},{2,3},{3,4},{4,5},{5,6},{6,7},{8,9},{9,10},{10,11},{11... | collective-permute-start | bytes 9320 | tf_op jit(solution)/shard_map/ppermute | solution.py:29
  164.6 4.0 %collective-permute-start.9 = (f32[4,1,96]{1,2,0:T(8,128)S(1)}, f32[4,1,96]{1,2,0:T(8,128)S(1)}, u32[]{:S(2)}, u32[]{:S(2)}) collective-permute-start(f32[4,1,96]{1,2,0:T(8,128)S(1)} %get-tuple-element.38), channel_id=1, source_target_pairs={{0,8},{8,16},{16,24},{1,9},{9,17},{17,25},{2,10},{10,18},{18,26},{... | collective-permute-start | bytes 4616 | tf_op jit(solution)/shard_map/ppermute | solution.py:29
  171.0 4.8 %collective-permute-start.11 = (f32[4,194,1]{1,2,0:T(1,128)S(1)}, f32[4,194,1]{1,2,0:T(1,128)S(1)}, u32[]{:S(2)}, u32[]{:S(2)}) collective-permute-start(f32[4,194,1]{1,2,0:T(1,128)S(1)} %get-tuple-element.29), channel_id=1, source_target_pairs={{0,1},{1,2},{2,3},{3,4},{4,5},{5,6},{6,7},{8,9},{9,10},{10,11},{11... | collective-permute-start | bytes 9320 | tf_op jit(solution)/shard_map/ppermute | solution.py:29
  179.2 6.8 %collective-permute-start.13 = (f32[4,1,96]{1,2,0:T(8,128)S(1)}, f32[4,1,96]{1,2,0:T(8,128)S(1)}, u32[]{:S(2)}, u32[]{:S(2)}) collective-permute-start(f32[4,1,96]{1,2,0:T(8,128)S(1)} %get-tuple-element.36), channel_id=1, source_target_pairs={{0,8},{8,16},{16,24},{1,9},{9,17},{17,25},{2,10},{10,18},{18,26},{... | collective-permute-start | bytes 4616 | tf_op jit(solution)/shard_map/ppermute | solution.py:29
  187.2 1.3 collective-permute-start.14
  188.5 5.7 %collective-permute-start.15 = (f32[4,194,1]{1,2,0:T(1,128)S(1)}, f32[4,194,1]{1,2,0:T(1,128)S(1)}, u32[]{:S(2)}, u32[]{:S(2)}) collective-permute-start(f32[4,194,1]{1,2,0:T(1,128)S(1)} %get-tuple-element.27), channel_id=1, source_target_pairs={{0,1},{1,2},{2,3},{3,4},{4,5},{5,6},{6,7},{8,9},{9,10},{10,11},{11... | collective-permute-start | bytes 9320 | tf_op jit(solution)/shard_map/ppermute | solution.py:29
  196.1 12.3 %all-to-all-start.1 = ((s32[1,32,9]{2,0,1:T(1,128)}), s32[1,32,9]{2,0,1:T(1,128)S(1)}, u32[]{:S(2)}, u32[]{:S(2)}) async-start(s32[1,32,9]{2,0,1:T(1,128)} %bitcast.15), calls=%async_computation.1 | async-start | bytes 32768 | tf_op jit(solution)/shard_map/all_to_all | solution.py:128
  211.2 15.1 %scatter_fusion = f32[4,288,128]{2,0,1:T(4,128)} fusion(f32[4,288,128]{2,0,1:T(4,128)} %broadcast_in_dim.7, s32[144]{0:T(256)S(1)} %bitcast.84, f32[144,4,128]{2,1,0:T(4,128)S(1)} %copy.63), kind=kCustom, calls=%fused_computation.1 | custom fusion | bytes 885312 | tf_op jit(solution)/shard_map/scatter | solution.py:113
  226.3 6.1 %all-to-all-start = ((f32[4,32,1152]{2,0,1:T(4,128)}), f32[4,32,1152]{2,0,1:T(4,128)}, u32[]{:S(2)}, u32[]{:S(2)}) async-start(f32[4,32,1152]{2,0,1:T(4,128)} %bitcast.77), calls=%async_computation | async-start | bytes 1179648 | tf_op jit(solution)/shard_map/all_to_all | solution.py:121
  233.9 16.1 %all-to-all-done = f32[4,32,1152]{2,0,1:T(4,128)} async-done(((f32[4,32,1152]{2,0,1:T(4,128)}), f32[4,32,1152]{2,0,1:T(4,128)}, u32[]{:S(2)}, u32[]{:S(2)}) %all-to-all-start) | async-done | bytes 589856 | tf_op jit(solution)/shard_map/all_to_all | solution.py:121
  250.0 1.9 copy.66
  251.9 1.9 reshape.124
  253.9 1.4 fusion.2
  255.4 5.5 %convolution_bitcast_fusion = f32[4,41,4096]{2,1,0:T(8,128)S(1)} fusion(f32[4,41,4096]{2,0,1:T(4,128)S(1)} %add_dynamic-update-slice_fusion, f32[41,41]{1,0:T(8,128)S(1)} %copy-done), kind=kOutput, calls=%fused_computation.3 | convolution fusion | flops 330498048 | bytes 5380676 | tf_op jit(solution)/shard_map/lk,fkc->flc/dot_general | solution.py:154
  260.9 1.6 copy-done.2
  263.5 2.6 all-to-all-start.2
  267.1 5.1 %copy.71 = f32[4,41,4096]{2,0,1:T(4,128)} copy(f32[4,41,4096]{2,1,0:T(8,128)} %copy-done.2) | data formatting | bytes 5373952
  272.2 1.7 all-to-all-done.2
  (101 shorter events, 28.5 us)
Async XLA Ops:
  7.2 248.2 %copy-start = (f32[41,41]{1,0:T(8,128)S(1)}, f32[41,41]{1,0:T(8,128)}, u32[]{:S(2)}) copy-start(f32[41,41]{1,0:T(8,128)} %param.21) | copy-start | bytes 20176
  7.2 140.6 %all-reduce.3.cloned.1.call-start = ((), (), s32[]{:S(2)}) async-start(), calls=%async_computation.3 | async-start | bytes 2359296 | tf_op jit(solution)/shard_map/psum | solution.py:19
  9.8 6.6 %collective-permute-start = (f32[4,1,96]{1,2,0:T(8,128)S(1)}, f32[4,1,96]{1,2,0:T(8,128)S(1)}, u32[]{:S(2)}, u32[]{:S(2)}) collective-permute-start(f32[4,1,96]{1,2,0:T(8,128)S(1)} %copy.47), channel_id=1, source_target_pairs={{8,0},{16,8},{24,16},{9,1},{17,9},{25,17},{10,2},{18,10},{26,18},{... | collective-permute-start | bytes 4616 | tf_op jit(solution)/shard_map/ppermute | solution.py:30
  11.2 5.2 %collective-permute-start.1 = (f32[4,1,96]{1,2,0:T(8,128)S(1)}, f32[4,1,96]{1,2,0:T(8,128)S(1)}, u32[]{:S(2)}, u32[]{:S(2)}) collective-permute-start(f32[4,1,96]{1,2,0:T(8,128)S(1)} %copy.49), channel_id=1, source_target_pairs={{0,8},{8,16},{16,24},{1,9},{9,17},{17,25},{2,10},{10,18},{18,26},{... | collective-permute-start | bytes 4616 | tf_op jit(solution)/shard_map/ppermute | solution.py:29
  16.5 6.8 %collective-permute-start.2 = (f32[4,194,1]{1,2,0:T(1,128)S(1)}, f32[4,194,1]{1,2,0:T(1,128)S(1)}, u32[]{:S(2)}, u32[]{:S(2)}) collective-permute-start(f32[4,194,1]{1,2,0:T(1,128)S(1)} %get-tuple-element.32), channel_id=1, source_target_pairs={{1,0},{2,1},{3,2},{4,3},{5,4},{6,5},{7,6},{9,8},{10,9},{11,10},{12... | collective-permute-start | bytes 9320 | tf_op jit(solution)/shard_map/ppermute | solution.py:30
  17.8 6.8 %collective-permute-start.3 = (f32[4,194,1]{1,2,0:T(1,128)S(1)}, f32[4,194,1]{1,2,0:T(1,128)S(1)}, u32[]{:S(2)}, u32[]{:S(2)}) collective-permute-start(f32[4,194,1]{1,2,0:T(1,128)S(1)} %get-tuple-element.33), channel_id=1, source_target_pairs={{0,1},{1,2},{2,3},{3,4},{4,5},{5,6},{6,7},{8,9},{9,10},{10,11},{11... | collective-permute-start | bytes 9320 | tf_op jit(solution)/shard_map/ppermute | solution.py:29
  23.3 130.9 %copy-start.7 = (s32[144,1]{0,1:T(1,128)S(1)}, s32[144,1]{0,1:T(1,128)}, u32[]{:S(2)}) copy-start(s32[144,1]{0,1:T(1,128)} %param.17) | copy-start | bytes 1732
  149.9 4.4 %collective-permute-start.4 = (f32[4,1,96]{1,2,0:T(8,128)S(1)}, f32[4,1,96]{1,2,0:T(8,128)S(1)}, u32[]{:S(2)}, u32[]{:S(2)}) collective-permute-start(f32[4,1,96]{1,2,0:T(8,128)S(1)} %get-tuple-element.41), channel_id=1, source_target_pairs={{8,0},{16,8},{24,16},{9,1},{17,9},{25,17},{10,2},{18,10},{26,18},{... | collective-permute-start | bytes 4616 | tf_op jit(solution)/shard_map/ppermute | solution.py:30
  151.2 4.1 %collective-permute-start.5 = (f32[4,1,96]{1,2,0:T(8,128)S(1)}, f32[4,1,96]{1,2,0:T(8,128)S(1)}, u32[]{:S(2)}, u32[]{:S(2)}) collective-permute-start(f32[4,1,96]{1,2,0:T(8,128)S(1)} %get-tuple-element.40), channel_id=1, source_target_pairs={{0,8},{8,16},{16,24},{1,9},{9,17},{17,25},{2,10},{10,18},{18,26},{... | collective-permute-start | bytes 4616 | tf_op jit(solution)/shard_map/ppermute | solution.py:29
  155.4 6.5 %collective-permute-start.6 = (f32[4,194,1]{1,2,0:T(1,128)S(1)}, f32[4,194,1]{1,2,0:T(1,128)S(1)}, u32[]{:S(2)}, u32[]{:S(2)}) collective-permute-start(f32[4,194,1]{1,2,0:T(1,128)S(1)} %get-tuple-element.30), channel_id=1, source_target_pairs={{1,0},{2,1},{3,2},{4,3},{5,4},{6,5},{7,6},{9,8},{10,9},{11,10},{12... | collective-permute-start | bytes 9320 | tf_op jit(solution)/shard_map/ppermute | solution.py:30
  156.7 5.9 %collective-permute-start.7 = (f32[4,194,1]{1,2,0:T(1,128)S(1)}, f32[4,194,1]{1,2,0:T(1,128)S(1)}, u32[]{:S(2)}, u32[]{:S(2)}) collective-permute-start(f32[4,194,1]{1,2,0:T(1,128)S(1)} %get-tuple-element.31), channel_id=1, source_target_pairs={{0,1},{1,2},{2,3},{3,4},{4,5},{5,6},{6,7},{8,9},{9,10},{10,11},{11... | collective-permute-start | bytes 9320 | tf_op jit(solution)/shard_map/ppermute | solution.py:29
  163.1 45.3 %copy-start.5 = (f32[192,96]{1,0:T(8,128)S(1)}, f32[192,96]{1,0:T(8,128)}, u32[]{:S(2)}) copy-start(f32[192,96]{1,0:T(8,128)} %param.13) | copy-start | bytes 221188
  163.3 5.6 %collective-permute-start.8 = (f32[4,1,96]{1,2,0:T(8,128)S(1)}, f32[4,1,96]{1,2,0:T(8,128)S(1)}, u32[]{:S(2)}, u32[]{:S(2)}) collective-permute-start(f32[4,1,96]{1,2,0:T(8,128)S(1)} %get-tuple-element.39), channel_id=1, source_target_pairs={{8,0},{16,8},{24,16},{9,1},{17,9},{25,17},{10,2},{18,10},{26,18},{... | collective-permute-start | bytes 4616 | tf_op jit(solution)/shard_map/ppermute | solution.py:30
  164.6 5.1 %collective-permute-start.9 = (f32[4,1,96]{1,2,0:T(8,128)S(1)}, f32[4,1,96]{1,2,0:T(8,128)S(1)}, u32[]{:S(2)}, u32[]{:S(2)}) collective-permute-start(f32[4,1,96]{1,2,0:T(8,128)S(1)} %get-tuple-element.38), channel_id=1, source_target_pairs={{0,8},{8,16},{16,24},{1,9},{9,17},{17,25},{2,10},{10,18},{18,26},{... | collective-permute-start | bytes 4616 | tf_op jit(solution)/shard_map/ppermute | solution.py:29
  169.7 6.2 %collective-permute-start.10 = (f32[4,194,1]{1,2,0:T(1,128)S(1)}, f32[4,194,1]{1,2,0:T(1,128)S(1)}, u32[]{:S(2)}, u32[]{:S(2)}) collective-permute-start(f32[4,194,1]{1,2,0:T(1,128)S(1)} %get-tuple-element.28), channel_id=1, source_target_pairs={{1,0},{2,1},{3,2},{4,3},{5,4},{6,5},{7,6},{9,8},{10,9},{11,10},{12... | collective-permute-start | bytes 9320 | tf_op jit(solution)/shard_map/ppermute | solution.py:30
  171.0 6.2 %collective-permute-start.11 = (f32[4,194,1]{1,2,0:T(1,128)S(1)}, f32[4,194,1]{1,2,0:T(1,128)S(1)}, u32[]{:S(2)}, u32[]{:S(2)}) collective-permute-start(f32[4,194,1]{1,2,0:T(1,128)S(1)} %get-tuple-element.29), channel_id=1, source_target_pairs={{0,1},{1,2},{2,3},{3,4},{4,5},{5,6},{6,7},{8,9},{9,10},{10,11},{11... | collective-permute-start | bytes 9320 | tf_op jit(solution)/shard_map/ppermute | solution.py:29
  177.9 8.2 %collective-permute-start.12 = (f32[4,1,96]{1,2,0:T(8,128)S(1)}, f32[4,1,96]{1,2,0:T(8,128)S(1)}, u32[]{:S(2)}, u32[]{:S(2)}) collective-permute-start(f32[4,1,96]{1,2,0:T(8,128)S(1)} %get-tuple-element.37), channel_id=1, source_target_pairs={{8,0},{16,8},{24,16},{9,1},{17,9},{25,17},{10,2},{18,10},{26,18},{... | collective-permute-start | bytes 4616 | tf_op jit(solution)/shard_map/ppermute | solution.py:30
  179.2 7.9 %collective-permute-start.13 = (f32[4,1,96]{1,2,0:T(8,128)S(1)}, f32[4,1,96]{1,2,0:T(8,128)S(1)}, u32[]{:S(2)}, u32[]{:S(2)}) collective-permute-start(f32[4,1,96]{1,2,0:T(8,128)S(1)} %get-tuple-element.36), channel_id=1, source_target_pairs={{0,8},{8,16},{16,24},{1,9},{9,17},{17,25},{2,10},{10,18},{18,26},{... | collective-permute-start | bytes 4616 | tf_op jit(solution)/shard_map/ppermute | solution.py:29
  187.2 21.4 %collective-permute-start.14 = (f32[4,194,1]{1,2,0:T(1,128)S(1)}, f32[4,194,1]{1,2,0:T(1,128)S(1)}, u32[]{:S(2)}, u32[]{:S(2)}) collective-permute-start(f32[4,194,1]{1,2,0:T(1,128)S(1)} %get-tuple-element.26), channel_id=1, source_target_pairs={{1,0},{2,1},{3,2},{4,3},{5,4},{6,5},{7,6},{9,8},{10,9},{11,10},{12... | collective-permute-start | bytes 9320 | tf_op jit(solution)/shard_map/ppermute | solution.py:30
  188.5 20.1 %collective-permute-start.15 = (f32[4,194,1]{1,2,0:T(1,128)S(1)}, f32[4,194,1]{1,2,0:T(1,128)S(1)}, u32[]{:S(2)}, u32[]{:S(2)}) collective-permute-start(f32[4,194,1]{1,2,0:T(1,128)S(1)} %get-tuple-element.27), channel_id=1, source_target_pairs={{0,1},{1,2},{2,3},{3,4},{4,5},{5,6},{6,7},{8,9},{9,10},{10,11},{11... | collective-permute-start | bytes 9320 | tf_op jit(solution)/shard_map/ppermute | solution.py:29
  196.1 30.2 %all-to-all-start.1 = ((s32[1,32,9]{2,0,1:T(1,128)}), s32[1,32,9]{2,0,1:T(1,128)S(1)}, u32[]{:S(2)}, u32[]{:S(2)}) async-start(s32[1,32,9]{2,0,1:T(1,128)} %bitcast.15), calls=%async_computation.1 | async-start | bytes 32768 | tf_op jit(solution)/shard_map/all_to_all | solution.py:128
  211.2 44.2 %copy-start.1 = (f32[4,41,4096]{2,0,1:T(4,128)S(1)}, f32[4,41,4096]{2,0,1:T(4,128)}, u32[]{:S(2)}) copy-start(f32[4,41,4096]{2,0,1:T(4,128)} %param.20) | copy-start | bytes 8060932
  226.3 23.7 %all-to-all-start = ((f32[4,32,1152]{2,0,1:T(4,128)}), f32[4,32,1152]{2,0,1:T(4,128)}, u32[]{:S(2)}, u32[]{:S(2)}) async-start(f32[4,32,1152]{2,0,1:T(4,128)} %bitcast.77), calls=%async_computation | async-start | bytes 1179648 | tf_op jit(solution)/shard_map/all_to_all | solution.py:121
  263.5 10.4 %all-to-all-start.2 = ((f32[32,1,1152]{2,1,0:T(1,128)}), f32[32,1,1152]{2,1,0:T(1,128)S(1)}, u32[]{:S(2)}, u32[]{:S(2)}) async-start(f32[32,1,1152]{2,1,0:T(1,128)} %bitcast.21), calls=%async_computation.2 | async-start | bytes 294912 | tf_op jit(solution)/shard_map/all_to_all | solution.py:161
  (5 other events, 56.1 us)
Sparse Core Ops, SparseCore 0:
  14.0 133.7 all-reduce.2
where the time goes:
time: 283 us; the launch traced here: 282 us
  waiting for transfers between devices  147 us (52%)
  starting transfers between devices  68.9 us (24%)
  local copies, waits for them, and re-layouts  34.6 us (12%)
  between operations  16.7 us (6%)
  matrix products  9.96 us (4%)
  other arithmetic  4.88 us (2%)
    psum x1, waiting for transfers between devices, spread(): return lax.psum(jnp.where(mine, value, jnp.zeros_like(value)), axis)  123 us
    ppermute x8, starting transfers between devices, extended(): before = lax.ppermute(last, axis, up)  37.5 us
    all_to_all x1, waiting for transfers between devices, on_device(): lax.all_to_all(send_flux.reshape(FIELDS, devices, capacity * EXCHANGE_PAT...  16.1 us
    scatter x1, local copies, waits for them, and re-layouts, on_device(): send_flux = jnp.zeros((FIELDS, devices * capacity, EXCHANGE_PATCH), jnp.f...  15.1 us
    all_to_all x1, starting transfers between devices, on_device(): lax.all_to_all(send_slot.reshape(1, devices, capacity), ('gx', 'gy'), spl...  12.3 us
    ppermute x8, starting transfers between devices, extended(): after = lax.ppermute(initial, axis, down)  10.3 us
    unnamed x22, local copies, waits for them, and re-layouts  8.48 us
    all_to_all x1, starting transfers between devices, on_device(): lax.all_to_all(send_flux.reshape(FIELDS, devices, capacity * EXCHANGE_PAT...  6.13 us
  transfers between devices with their start and end apart: 20, of which 9 were waited for; matrix products, arithmetic and copies ran while one was open for 10% of the time, Pallas kernels for 0%

commit v1 on v0

v1 whole, which is shorter than its diff:
```python
import functools
import math

import jax
import jax.numpy as jnp
from jax import lax
from jax.experimental import pallas as pl
from jax.experimental.pallas import tpu as pltpu
from jax.sharding import PartitionSpec as P

FIELDS = 4
PATCH = 128
MARINE = 32
STEPS = 4
WROWS = 48
WCOLS = 32
HALO = 8
CHUNK = 256
DIFFUSE = 0.24
RELAX = 0.3
DRAG = 0.5
F32 = jnp.float32
BF16 = jnp.bfloat16
MESH = pl.DeviceIdType.MESH
NT = (((1,), (1,)), ((), ()))
TN = (((0,), (0,)), ((), ()))


def iota(shape, dim):
    return lax.broadcasted_iota(jnp.int32, shape, dim)


def hot(condition):
    return jnp.where(condition, 1.0, 0.0).astype(BF16)


def dot(a, b):
    return jnp.dot(a, b, preferred_element_type=F32)


def first_parent(first_fine):
    return (4 * first_fine - 11) // 26


def kernel(
    nx, ny, cap, jp, rp, yw,
    holder, corner, index_row, owner_col, fine, skin, coarse, exchange, marine, op,
    nest_out, marine_out, heat_out,
    centre, strips, rows_in, cols_in, corners_in,
    tx1, rx1, pmat, flux_tile, flux_rows, flux_pack, tx2, rx2, amat, qmat, tx3, rx3,
    marine_in, mixed, skin_base, coarse_rows,
    marine_sem, out_sem, local_sem, halo_send, halo_recv, send_sem, recv_sem,
):
    tile_x, tile_y = fine.shape[1], fine.shape[2]
    blocks = owner_col.shape[0]
    devices = nx * ny
    ix, iy = lax.axis_index("gx"), lax.axis_index("gy")
    me = ix * ny + iy

    barrier = pltpu.get_barrier_semaphore()

    def greet(t, carry):
        other = lax.rem(me + t, devices)
        pl.semaphore_signal(
            barrier, inc=1, device_id=(lax.div(other, ny), lax.rem(other, ny)), device_id_type=MESH
        )
        return carry

    lax.fori_loop(1, devices, greet, 0)
    marine_copy = pltpu.make_async_copy(marine, marine_in, marine_sem)
    marine_copy.start()

    for f in range(FIELDS):
        centre[f, :, :] = jnp.zeros((tile_x, PATCH), F32)
        centre[f, :, 0:tile_y] = fine[f]
    wide = jnp.concatenate([centre[f].astype(BF16) for f in range(FIELDS)], axis=1)
    r = iota((32, FIELDS * PATCH), 0)
    field_col = ((r & 15) >> 2) * PATCH + (r & 3)
    lane = iota((32, FIELDS * PATCH), 1)
    pick = hot(lane == field_col + jnp.where(r >= 16, tile_y - 4, 0))
    place = hot(lane == field_col + jnp.where(r >= 16, tile_y, PATCH - 4))
    wide = jnp.concatenate([wide, jnp.zeros((256 - tile_x, FIELDS * PATCH), BF16)], axis=0)
    strips[...] = lax.dot_general(pick, wide, NT, preferred_element_type=F32).astype(BF16)

    owner_row, pos_row = index_row[0:1, :], index_row[1:2, :]
    same = owner_col[...] == owner_row
    k0, k1 = iota((blocks, 256), 0), iota((blocks, 256), 1)
    rank_row = jnp.sum(jnp.where(same & (k0 < k1), 1.0, 0.0), axis=0, keepdims=True).astype(jnp.int32)
    rank_col = jnp.sum(jnp.where(same & (k1 < k0), 1.0, 0.0), axis=1, keepdims=True).astype(jnp.int32)

    owners_hot = jnp.where(iota((devices, 256), 0) == owner_row, 1.0, 0.0)
    weighted = (owners_hot * (pos_row + 1).astype(F32)).astype(BF16)
    j = iota((PATCH, 256), 0)
    field = sum([jnp.where(j >= n * cap, 1, 0) for n in range(1, FIELDS)])
    ranks_hot = hot((j - field * cap == rank_row) & (j < FIELDS * cap))
    slots = lax.dot_general(weighted, ranks_hot, NT, preferred_element_type=F32)
    j = iota((devices, PATCH), 1)
    field = sum([jnp.where(j >= n * cap, 1.0, 0.0) for n in range(1, FIELDS)])
    codes = jnp.where(slots > 0.5, slots + MARINE * field, 0.0)

    cells = coarse.shape[1]
    away = (holder[0] - me) * 65536
    q = iota((cells, yw), 0)
    choose_y = hot(q == iota((cells, yw), 1) + (corner[1] - 1))
    p = iota((WROWS, cells), 1) - iota((WROWS, cells), 0) - (corner[0] + away)
    choose_x = jnp.concatenate([hot(p == first_parent(a * tile_x - 3)) for a in range(nx)], axis=0)
    windows = []
    for f in range(FIELDS):
        narrow = dot(coarse[f], choose_y).astype(BF16)
        windows.append(dot(choose_x, narrow))
    lane_group = iota((nx * WROWS, PATCH), 1) // WCOLS
    piece_row = iota((WROWS, PATCH), 0)
    for b in range(ny):
        base = first_parent(b * tile_y - 3) + 1
        piece = jnp.zeros((nx * WROWS, PATCH), F32)
        for f in range(FIELDS):
            moved = pltpu.roll(windows[f], (f * WCOLS - base) % yw, 1)[:, 0:PATCH]
            piece = jnp.where(lane_group == f, moved, piece)
        for a in range(nx):
            d = a * ny + b
            part = piece[a * WROWS : (a + 1) * WROWS]
            tx1[d] = jnp.where(piece_row == WROWS - 1, codes[d : d + 1, :], part).astype(BF16)

    pl.semaphore_wait(barrier, devices - 1)

    def send(phase, source, target):
        def one(t, carry):
            other = lax.rem(me + t, devices)
            pltpu.make_async_remote_copy(
                src_ref=source(other),
                dst_ref=target,
                send_sem=send_sem.at[phase],
                recv_sem=recv_sem.at[phase],
                device_id=(lax.div(other, ny), lax.rem(other, ny)),
                device_id_type=MESH,
            ).start()
            return carry

        lax.fori_loop(1, devices, one, 0)

    def all_of(ref, rows, sem):
        whole = ref.at[pl.ds(0, (devices - 1) * rows)]
        pltpu.make_async_copy(whole, whole, sem).wait()

    west, east = lax.rem(ix + nx - 1, nx), lax.rem(ix + 1, nx)
    south, north = lax.rem(iy + ny - 1, ny), lax.rem(iy + 1, ny)
    left, right = pl.ds(0, 16), pl.ds(16, 16)
    low, high = pl.ds(0, 128), pl.ds(128, 128)
    halos = [
        (centre.at[:, pl.ds(tile_x - HALO, HALO), :], rows_in.at[0], (east, iy)),
        (centre.at[:, pl.ds(0, HALO), :], rows_in.at[1], (west, iy)),
        (strips.at[right], cols_in.at[left], (ix, north)),
        (strips.at[left], cols_in.at[right], (ix, south)),
        (strips.at[right, high], corners_in.at[0, left], (east, north)),
        (strips.at[left, high], corners_in.at[0, right], (east, south)),
        (strips.at[right, low], corners_in.at[1, left], (west, north)),
        (strips.at[left, low], corners_in.at[1, right], (west, south)),
    ]
    halos = [
        pltpu.make_async_remote_copy(
            src_ref=src, dst_ref=dst, send_sem=halo_send.at[n], recv_sem=halo_recv.at[n],
            device_id=where, device_id_type=MESH,
        )
        for n, (src, dst, where) in enumerate(halos)
    ]
    for copy in halos:
        copy.start()
    send(0, lambda other: tx1.at[other], rx1.at[me])
    own1 = pltpu.make_async_copy(tx1.at[me], rx1.at[me], local_sem)
    own1.start()

    target = owner_row * jp + rank_row

    def dispatch_rows(c, carry):
        start = pl.multiple_of(c * CHUNK, CHUNK)
        row = iota((CHUNK, 256), 0) + start
        for f in range(FIELDS):
            pmat[pl.ds(start, CHUNK), f * 256 : (f + 1) * 256] = hot(row == target + f * cap)
        return carry

    lax.fori_loop(0, devices * jp // CHUNK, dispatch_rows, 0)
    flux_pack[...] = jnp.zeros(flux_pack.shape, BF16)

    op_high = op[...].astype(BF16)
    op_low = (op[...] - op_high.astype(F32)).astype(BF16)
    marine_copy.wait()
    width = 512
    for f in range(FIELDS):

        def mix(c, carry, f=f):
            columns = pl.ds(pl.multiple_of(c * width, width), width)
            value = marine_in[f, :, columns]
            m_high = value.astype(BF16)
            m_low = (value - m_high.astype(F32)).astype(BF16)
            mixed[f, :, columns] = dot(op_high, m_high) + (dot(op_low, m_high) + dot(op_high, m_low))
            return carry

        lax.fori_loop(0, marine_in.shape[2] // width, mix, 0)
    for g in range(MARINE):
        skin_base[g : g + 1, :] = mixed[0, 0:1, g * PATCH : (g + 1) * PATCH]
        for f in range(FIELDS):
            coarse_rows[f * MARINE + g : f * MARINE + g + 1, :] = exchange[f : f + 1, g * PATCH : (g + 1) * PATCH]

    own1.wait()
    all_of(rx1, 1, recv_sem.at[0])
    for copy in halos:
        copy.wait()
    all_of(tx1, 1, send_sem.at[0])

    window = lax.fori_loop(
        0, devices, lambda s, total: total + rx1[s].astype(F32), jnp.zeros((WROWS, PATCH), F32)
    ).astype(BF16)
    height = tile_x + 2 * HALO
    fx = (iota((height, WROWS), 0) + (ix * tile_x - HALO)).astype(F32)
    first_x = (4 * (ix * tile_x - 3) - 11 + 26) // 26 - 1
    at_x = (fx + 0.5) * (2.0 / 13.0) - 0.5 + corner[0].astype(F32)
    px = (iota((height, WROWS), 1) + (first_x + corner[0])).astype(F32)
    wx = jnp.maximum(0.0, 1.0 - jnp.abs(at_x - px)).astype(BF16)
    lane_y = iota((PATCH, PATCH), 0)
    lane_y = lane_y - jnp.where(lane_y >= PATCH - 16, PATCH, 0)
    fy = (lane_y + iy * tile_y).astype(F32)
    first_y = (4 * (iy * tile_y - 3) - 11 + 26) // 26 - 1
    at_y = (fy + 0.5) * (2.0 / 13.0) - 0.5 + corner[1].astype(F32)
    py = ((iota((PATCH, PATCH), 1) & (WCOLS - 1)) + (first_y + corner[1])).astype(F32)
    wy = jnp.maximum(0.0, 1.0 - jnp.abs(at_y - py))
    group_y = iota((PATCH, PATCH), 1) // WCOLS

    side = lax.dot_general(cols_in[...], place, TN, preferred_element_type=F32)
    side_low = lax.dot_general(corners_in[0], place, TN, preferred_element_type=F32)
    side_high = lax.dot_general(corners_in[1], place, TN, preferred_element_type=F32)

    gi = iota((height, PATCH), 0) + (ix * tile_x - HALO)
    gj = iota((height, PATCH), 1)
    gj = gj - jnp.where(gj >= PATCH - 16, PATCH, 0) + iy * tile_y
    inside = (gi >= 0) & (gi < nx * tile_x) & (gj >= 0) & (gj < ny * tile_y)
    final = []
    for f in range(FIELDS):
        wy_f = jnp.where(group_y == f, wy, 0.0).astype(BF16)
        partial = lax.dot_general(window, wy_f, NT, preferred_element_type=F32).astype(BF16)
        forcing = dot(wx, partial)
        cut = slice(f * PATCH, (f + 1) * PATCH)
        state = jnp.concatenate(
            [
                rows_in[0, f] + side_low[56:64, cut],
                centre[f] + side[0:tile_x, cut],
                rows_in[1, f] + side_high[0:8, cut],
            ],
            axis=0,
        )
        state = jnp.where(inside, state, 0.0)
        for _ in range(STEPS):
            beside = (
                pltpu.roll(state, 1, 0) + pltpu.roll(state, height - 1, 0)
                + pltpu.roll(state, 1, 1) + pltpu.roll(state, PATCH - 1, 1)
            )
            state = state + DIFFUSE * (beside - 4.0 * state) + RELAX * (forcing - state)
            state = jnp.where(inside, state, 0.0)
        state = state[HALO : HALO + tile_x]
        nest_out[f] = state[:, 0:tile_y]
        final.append(state)

    flux_tile[:, 0:tile_y] = skin[...]
    heat = flux_tile[...]
    u, v, ta, qa = final
    drag = DRAG * jnp.sqrt(1.0 + u * u + v * v)
    lane = iota((tile_x // 4, PATCH), 1)
    for f, flux in enumerate((drag * (ta - heat), drag * (qa - 0.5 * heat), drag * u, drag * v)):
        flux_tile[...] = flux
        f0, f1, f2, f3 = [flux_tile[pl.ds(n, tile_x // 4, stride=4), :] for n in range(4)]
        f1, f2 = pltpu.roll(f1, 96, 1), pltpu.roll(f2, 64, 1)
        flux_rows[pl.ds(0, blocks // 3, stride=3), :] = jnp.where(lane < 96, f0, f1)
        flux_rows[pl.ds(1, blocks // 3, stride=3), :] = jnp.where(lane < 64, f1, f2)
        flux_rows[pl.ds(2, blocks // 3, stride=3), :] = jnp.where(lane < 32, f2, pltpu.roll(f3, 32, 1))
        flux_pack[f * 256 : f * 256 + blocks, :] = flux_rows[...].astype(BF16)

    def dispatch(c, carry):
        rows = pl.ds(pl.multiple_of(c * CHUNK, CHUNK), CHUNK)
        tx2[rows, :] = dot(pmat[rows, :], flux_pack[...]).astype(BF16)
        return carry

    lax.fori_loop(0, devices * jp // CHUNK, dispatch, 0)

    def part(ref, device, rows):
        return ref.at[pl.ds(pl.multiple_of(device * rows, 16), rows)]

    send(1, lambda other: part(tx2, other, jp), part(rx2, me, jp))
    own2 = pltpu.make_async_copy(part(tx2, me, jp), part(rx2, me, jp), local_sem)
    own2.start()

    got = rx1[:, WROWS - 16 : WROWS, :].astype(F32)[:, 15, :].astype(BF16)

    def spread_codes(pitch, limit):
        period = math.lcm(pitch, PATCH)
        a, b = iota((PATCH, period), 0), iota((PATCH, period), 1)
        repeat = functools.reduce(
            jnp.logical_or, [b == a + n * pitch for n in range(period // pitch)]
        ) & (a < limit)
        tiled = dot(got, hot(repeat))
        tiled = jnp.concatenate([tiled] * (devices * pitch // period), axis=1)
        s, l = iota(tiled.shape, 0), iota(tiled.shape, 1)
        mine = (l >= s * pitch) & (l < (s + 1) * pitch)
        return jnp.sum(jnp.where(mine, tiled, 0.0), axis=0, keepdims=True).astype(jnp.int32) - 1

    code = spread_codes(jp, FIELDS * cap)
    amat[...] = hot(iota((FIELDS * MARINE, devices * jp), 0) == code)
    count = jnp.sum(amat[0:MARINE, :].astype(F32), axis=1, keepdims=True)
    code = spread_codes(rp, cap)
    qmat[...] = hot(iota((MARINE, devices * rp), 0) == code)

    own2.wait()
    all_of(rx2, jp, recv_sem.at[1])
    all_of(tx2, jp, send_sem.at[1])
    sums = dot(amat[...], rx2[...])
    least = jnp.maximum(count, 1.0)
    empty = jnp.where(count == 0.0, 1.0, 0.0)
    forced = [
        (sums[f * MARINE : (f + 1) * MARINE] + coarse_rows[f * MARINE : (f + 1) * MARINE, :] * empty) / least
        for f in range(FIELDS)
    ]
    new_skin = (skin_base[...] + op[0:1, 0:1] * forced[0]).astype(BF16)
    tx3[...] = lax.dot_general(qmat[...], new_skin, TN, preferred_element_type=F32).astype(BF16)
    send(2, lambda other: part(tx3, other, rp), part(rx3, me, rp))
    own3 = pltpu.make_async_copy(part(tx3, me, rp), part(rx3, me, rp), local_sem)
    own3.start()

    first = op[:, 0:1]
    for f in range(FIELDS):
        for g in range(MARINE):
            cut = slice(g * PATCH, (g + 1) * PATCH)
            mixed[f, :, cut] = mixed[f, :, cut] + first * forced[f][g : g + 1, :]
    marine_back = pltpu.make_async_copy(mixed, marine_out, out_sem)
    marine_back.start()
    where_from = hot(iota((blocks, devices * rp), 1) == owner_col[...] * rp + rank_col)
    own3.wait()
    all_of(rx3, rp, recv_sem.at[2])
    all_of(tx3, rp, send_sem.at[2])
    heat_out[...] = dot(where_from, rx3[...])
    marine_back.wait()


def on_device(nx, ny, fine, skin, coarse, holder, corner, owner, position, exchange, marine, op):
    devices = nx * ny
    tile_x, tile_y = fine.shape[1:]
    blocks = tile_x * tile_y // PATCH
    cap = max(2, (2 * blocks + devices - 1) // devices)
    jp = -(-FIELDS * cap // 16) * 16
    rp = -(-cap // 16) * 16
    last = first_parent((ny - 1) * tile_y - 3) + 1 + 18
    yw = -(-last // PATCH) * PATCH
    layers, cells = marine.shape[1:]
    index_row = jnp.pad(
        jnp.stack([owner[:, 0], position]), ((0, 0), (0, 256 - blocks)), constant_values=-1
    )
    vmem = pl.BlockSpec(memory_space=pltpu.VMEM)
    smem = pl.BlockSpec(memory_space=pltpu.SMEM)
    anywhere = pl.BlockSpec(memory_space=pl.ANY)
    nest, marine_new, heat = pl.pallas_call(
        functools.partial(kernel, nx, ny, cap, jp, rp, yw),
        out_shape=(
            jax.ShapeDtypeStruct(fine.shape, F32),
            jax.ShapeDtypeStruct(marine.shape, F32),
            jax.ShapeDtypeStruct((blocks, PATCH), F32),
        ),
        in_specs=[smem, smem, vmem, vmem, vmem, vmem, vmem, vmem, anywhere, vmem],
        out_specs=(vmem, anywhere, vmem),
        scratch_shapes=[
            pltpu.VMEM((FIELDS, tile_x, PATCH), F32),
            pltpu.VMEM((32, 256), BF16),
            pltpu.VMEM((2, FIELDS, HALO, PATCH), F32),
            pltpu.VMEM((32, 256), BF16),
            pltpu.VMEM((2, 32, PATCH), BF16),
            pltpu.VMEM((devices, WROWS, PATCH), BF16),
            pltpu.VMEM((devices, WROWS, PATCH), BF16),
            pltpu.VMEM((devices * jp, FIELDS * 256), BF16),
            pltpu.VMEM((tile_x, PATCH), F32),
            pltpu.VMEM((blocks, PATCH), F32),
            pltpu.VMEM((FIELDS * 256, PATCH), BF16),
            pltpu.VMEM((devices * jp, PATCH), BF16),
            pltpu.VMEM((devices * jp, PATCH), BF16),
            pltpu.VMEM((FIELDS * MARINE, devices * jp), BF16),
            pltpu.VMEM((MARINE, devices * rp), BF16),
            pltpu.VMEM((devices * rp, PATCH), BF16),
            pltpu.VMEM((devices * rp, PATCH), BF16),
            pltpu.VMEM((FIELDS, layers, cells), F32),
            pltpu.VMEM((FIELDS, layers, cells), F32),
            pltpu.VMEM((MARINE, PATCH), F32),
            pltpu.VMEM((FIELDS * MARINE, PATCH), F32),
            pltpu.SemaphoreType.DMA,
            pltpu.SemaphoreType.DMA,
            pltpu.SemaphoreType.DMA,
            pltpu.SemaphoreType.DMA((8,)),
            pltpu.SemaphoreType.DMA((8,)),
            pltpu.SemaphoreType.DMA((3,)),
            pltpu.SemaphoreType.DMA((3,)),
        ],
        compiler_params=pltpu.CompilerParams(
            collective_id=0, has_side_effects=True, vmem_limit_bytes=40 * 1024 * 1024
        ),
    )(holder, corner, index_row, owner, fine, skin, coarse, exchange, marine, op)
    return nest, marine_new, heat.reshape(tile_x, tile_y)


def solution(mesh):
    in_specs = (
        P(None, "gx", "gy"),
        P("gx", "gy"),
        P(None, "gx", "gy"),
        P(),
        P(),
        P(("gx", "gy"), None),
        P(("gx", "gy")),
        P(None, ("gx", "gy")),
        P(None, None, ("gx", "gy")),
        P(),
    )
    out_specs = (P(None, "gx", "gy"), P(None, None, ("gx", "gy")), P("gx", "gy"))
    return jax.shard_map(
        functools.partial(on_device, mesh.shape["gx"], mesh.shape["gy"]),
        mesh=mesh,
        in_specs=in_specs,
        out_specs=out_specs,
        check_vma=False,
    )
```

time: 283 us -> 51.7 us (0.18)
  waiting for transfers between devices: 147 us -> 0 us
  starting transfers between devices: 68.9 us -> 0 us
  Pallas kernels: 0 us -> 38.2 us
  local copies, waits for them, and re-layouts: 34.6 us -> 11.1 us
  between operations: 16.7 us -> 1.38 us
  matrix products: 9.96 us -> 0 us
  other arithmetic: 4.88 us -> 0.7 us
    psum x1 -> x0, waiting for transfers between devices: 123 us -> none  [spread(): return lax.psum(jnp.where(mine, value, jnp.zeros_like(value)), axis)]
    ppermute x16 -> x0, starting transfers between devices: 47.9 us -> none  [the longest x8 37.5 us: extended(): before = lax.ppermute(last, axis, up)]
    pallas_call x0 -> x1, Pallas kernels: none -> 38.2 us  [on_device(): pl.pallas_call(functools.partial(kernel, nx, ny, cap, jp, rp, yw), out_sh...]
    all_to_all x3 -> x0, starting transfers between devices: 21 us -> none  [the longest x1 12.3 us: on_device(): lax.all_to_all(send_slot.reshape(1, devices, capacity), ('gx', 'gy'), spl...]
    all_to_all x3 -> x0, waiting for transfers between devices: 17.9 us -> none  [the longest x1 16.1 us: on_device(): lax.all_to_all(send_flux.reshape(FIELDS, devices, capacity * EXCHANGE_PAT...]
    scatter x2 -> x0, local copies, waits for them, and re-layouts: 16.3 us -> none  [the longest x1 15.1 us: on_device(): send_flux = jnp.zeros((FIELDS, devices * capacity, EXCHANGE_PATCH), jnp.f...]
    dot_general x4 -> x0, matrix products: 9.96 us -> none  [the longest x1 5.53 us: on_device(): jnp.einsum('lk,fkc->flc', diffusion_solver_operator, forced, precision=la...]
    ppermute x16 -> x0, waiting for transfers between devices: 6.05 us -> none  [the longest x8 6.03 us: extended(): before = lax.ppermute(last, axis, up)]
  transfers between devices with their start and end apart: 20 -> 0, of which waited for: 9 -> 0; matrix products, arithmetic and copies ran while one was open for 10% -> 0% of each run, Pallas kernels for 0% -> 0%
where the time goes in v1:
time: 51.7 us; the launch traced here: 51.5 us
  Pallas kernels  38.2 us (74%)
  local copies, waits for them, and re-layouts  11.1 us (21%)
  between operations  1.38 us (3%)
  other arithmetic  0.7 us (1%)
    pallas_call x1, Pallas kernels, on_device(): pl.pallas_call(functools.partial(kernel, nx, ny, cap, jp, rp, yw), out_sh...  38.2 us
    unnamed x20, local copies, waits for them, and re-layouts  9.52 us
    reshape x1, local copies, waits for them, and re-layouts, on_device(): return (nest, marine_new, heat.reshape(tile_x, tile_y))  1.61 us

profile of v1, /device:TPU:0, one launch (start us, length us, event | category | flops | bytes accessed | tf_op | source)
XLA Modules:
  0.0 51.5 jit_solution(14953229762775463796)
XLA Ops:
  1.3 0.7 %pad_add_fusion = s32[2,144]{1,0:T(2,128)S(1)} fusion(s32[1,144]{1,0:T(1,128)} %bitcast.3, s32[1,144]{1,0:T(1,128)} %bitcast.2), kind=kLoop, calls=%fused_computation | loop fusion | flops 288 | bytes 2304 | tf_op jit(solution)/shard_map/stack | solution.py:352
  2.0 1.4 %copy.13.owner_col = s32[144,1]{1,0:T(8,128)} copy(s32[144,1]{0,1:T(1,128)} %param.15) | data formatting | bytes 1152 | tf_op args[5]
  3.4 0.0 copy-start
  3.4 0.0 copy-start.1
  3.4 0.0 copy-start.2
  3.4 0.0 copy-start.3
  3.4 0.0 copy-start.5
  3.4 0.0 copy-start.6
  3.4 0.0 copy-start.7
  3.5 3.5 %copy.14.marine = f32[4,41,4096]{2,1,0:T(8,128)S(1)} copy(f32[4,41,4096]{2,0,1:T(4,128)} %param.18) | data formatting | bytes 5373952 | tf_op args[8]
  6.9 0.0 copy-done
  6.9 0.0 copy-done.1
  6.9 0.0 copy-done.2
  6.9 0.0 copy-done.3
  7.0 0.0 copy-done.5
  7.0 0.0 copy-done.6
  7.0 0.0 copy-done.7
  7.0 38.2 %shard_map.121 = (f32[4,192,96]{2,1,0:T(8,128)S(1)}, f32[4,41,4096]{2,1,0:T(8,128)S(1)}, f32[144,128]{1,0:T(8,128)S(1)}) custom-call(s32[1]{0:T(128)S(6)} %copy.17.holder, s32[2]{0:T(128)S(1)} %copy-done.7, s32[2,256]{1,0:T(2,128)S(1)} %pad.4.index_row, s32[144,1]{1,0:T(8,128)S(1)} %copy-done.2, f32[4,192,96]{2,1,0:T(8,128)S(1)} %copy-done.1, ...), custom_call_target="tpu_custom_call" | custom-call | tf_op jit(solution)/shard_map/pallas_call | solution.py:357
  45.2 0.0 copy-start.4
  45.2 0.6 %copy-done.4 = f32[144,128]{1,0:T(8,128)} copy-done((f32[144,128]{1,0:T(8,128)}, f32[144,128]{1,0:T(8,128)S(1)}, u32[]{:S(2)}) %copy-start.4) | copy-done | bytes 73752
  45.9 1.6 %reshape.9 = f32[192,96]{1,0:T(8,128)} reshape(f32[144,128]{1,0:T(8,128)} %copy-done.4) | data formatting | bytes 147456 | tf_op jit(solution)/shard_map/reshape | solution.py:400
  47.5 3.2 %copy.15 = f32[4,41,4096]{2,0,1:T(4,128)} copy(f32[4,41,4096]{2,1,0:T(8,128)S(1)} %get-tuple-element.10) | data formatting | bytes 5373952
  50.7 0.7 %copy.18 = f32[4,192,96]{2,1,0:T(8,128)} copy(f32[4,192,96]{2,1,0:T(8,128)S(1)} %get-tuple-element.15) | data formatting | bytes 589824
  (1 shorter events, 0.0 us)
Async XLA Ops:
  3.4 3.5 %copy-start = (bf16[4,384,384]{2,1,0:T(8,128)(2,1)S(1)}, bf16[4,384,384]{2,1,0:T(8,128)(2,1)}, u32[]{:S(2)}) copy-start(bf16[4,384,384]{2,1,0:T(8,128)(2,1)} %coarse.1) | copy-start | bytes 3538948
  3.4 3.5 %copy-start.1 = (f32[4,192,96]{2,1,0:T(8,128)S(1)}, f32[4,192,96]{2,1,0:T(8,128)}, u32[]{:S(2)}) copy-start(f32[4,192,96]{2,1,0:T(8,128)} %fine.1) | copy-start | bytes 884740
  3.4 3.5 %copy-start.2 = (s32[144,1]{1,0:T(8,128)S(1)}, s32[144,1]{1,0:T(8,128)}, u32[]{:S(2)}) copy-start(s32[144,1]{1,0:T(8,128)} %copy.13.owner_col) | copy-start | bytes 1732
  3.4 3.5 %copy-start.3 = (f32[192,96]{1,0:T(8,128)S(1)}, f32[192,96]{1,0:T(8,128)}, u32[]{:S(2)}) copy-start(f32[192,96]{1,0:T(8,128)} %skin.1) | copy-start | bytes 221188
  3.4 3.5 %copy-start.5 = (f32[4,4096]{1,0:T(4,128)S(1)}, f32[4,4096]{1,0:T(4,128)}, u32[]{:S(2)}) copy-start(f32[4,4096]{1,0:T(4,128)} %exchange.1) | copy-start | bytes 196612
  3.4 3.5 %copy-start.6 = (f32[41,41]{1,0:T(8,128)S(1)}, f32[41,41]{1,0:T(8,128)}, u32[]{:S(2)}) copy-start(f32[41,41]{1,0:T(8,128)} %op.1) | copy-start | bytes 20176
  3.4 3.5 %copy-start.7 = (s32[2]{0:T(128)S(1)}, s32[2]{0:T(128)}, u32[]{:S(2)}) copy-start(s32[2]{0:T(128)} %corner.1) | copy-start | bytes 28
  45.2 0.6 %copy-start.4 = (f32[144,128]{1,0:T(8,128)}, f32[144,128]{1,0:T(8,128)S(1)}, u32[]{:S(2)}) copy-start(f32[144,128]{1,0:T(8,128)S(1)} %get-tuple-element.8) | copy-start | bytes 221188

commit v2 on v1

v2 whole, which is shorter than its diff:
```python
import functools
import math

import jax
import jax.numpy as jnp
from jax import lax
from jax.experimental import pallas as pl
from jax.experimental.pallas import tpu as pltpu
from jax.sharding import PartitionSpec as P

FIELDS = 4
PATCH = 128
MARINE = 32
STEPS = 4
WCOLS = 32
SLOT_LANE = 18
HALO = 8
DIFFUSE = 0.24
RELAX = 0.3
DRAG = 0.5
F32 = jnp.float32
BF16 = jnp.bfloat16
MESH = pl.DeviceIdType.MESH
NT = (((1,), (1,)), ((), ()))
TN = (((0,), (0,)), ((), ()))


def iota(shape, dim):
    return lax.broadcasted_iota(jnp.int32, shape, dim)


def hot(condition):
    return jnp.where(condition, 1.0, 0.0).astype(BF16)


def dot(a, b):
    return jnp.dot(a, b, preferred_element_type=F32)


def first_parent(first_fine):
    return (4 * first_fine - 11) // 26


def kernel(
    nx, ny, cap, jp, rp, yw, wrows, per,
    holder, corner, owner, position, fine, skin, coarse_far, exchange, marine, op,
    nest_out, marine_out, heat_out,
    coarse, index_row, centre, strips, rows_in, cols_in, corners_in,
    tx1, rx1, pmat, flux_tile, flux_rows, flux_pack, tx2, rx2, amat, qmat, tx3, rx3,
    marine_in, mixed, op_column, coarse_rows, forced,
    marine_sem, out_sem, local_sem, halo_send, halo_recv, send_sem, recv_sem,
):
    tile_x, tile_y = fine.shape[1], fine.shape[2]
    blocks = owner.shape[1]
    layers = op.shape[0]
    devices = nx * ny
    ix, iy = lax.axis_index("gx"), lax.axis_index("gy")
    me = ix * ny + iy

    coarse_copy = pltpu.make_async_copy(coarse_far, coarse, local_sem.at[0])
    coarse_copy.start()
    rx3[...] = jnp.zeros(rx3.shape, F32)
    barrier = pltpu.get_barrier_semaphore()

    def greet(t, carry):
        other = lax.rem(me + t, devices)
        pl.semaphore_signal(
            barrier, inc=1, device_id=(lax.div(other, ny), lax.rem(other, ny)), device_id_type=MESH
        )
        return carry

    lax.fori_loop(1, devices, greet, 0)

    def ocean_block(ref, g):
        return ref.at[:, :, pl.ds(pl.multiple_of(g * PATCH, PATCH), PATCH)]

    def fetch(g):
        return pltpu.make_async_copy(
            ocean_block(marine, g), marine_in.at[g, :, pl.ds(0, FIELDS), :], marine_sem.at[g]
        )

    def keep(g):
        return pltpu.make_async_copy(
            mixed.at[g, :, pl.ds(0, FIELDS), :], ocean_block(marine_out, g), out_sem.at[g]
        )

    def each(count, work):
        def one(n, carry):
            work(n)
            return carry

        lax.fori_loop(0, count, one, 0)

    each(MARINE, lambda g: fetch(g).start())

    for f in range(FIELDS):
        centre[f, :, :] = jnp.zeros((tile_x, PATCH), F32)
        centre[f, :, 0:tile_y] = fine[f]
    wide = jnp.concatenate([centre[f].astype(BF16) for f in range(FIELDS)], axis=1)
    r = iota((32, FIELDS * PATCH), 0)
    field_col = ((r & 15) >> 2) * PATCH + (r & 3)
    lane = iota((32, FIELDS * PATCH), 1)
    pick = hot(lane == field_col + jnp.where(r >= 16, tile_y - 4, 0))
    place = hot(lane == field_col + jnp.where(r >= 16, tile_y, PATCH - 4))
    wide = jnp.concatenate([wide, jnp.zeros((256 - tile_x, FIELDS * PATCH), BF16)], axis=0)
    strips[...] = lax.dot_general(pick, wide, NT, preferred_element_type=F32).astype(BF16)

    index_row[...] = jnp.full(index_row.shape, -1, jnp.int32)
    index_row[0:1, 0:blocks] = owner[...]
    index_row[1:2, 0:blocks] = position[...]
    owner_row, pos_row = index_row[0:1, :], index_row[1:2, :]
    k0, k1 = iota((blocks, 256), 0), iota((blocks, 256), 1)
    owner_col = jnp.sum(
        jnp.where(k0 == k1, owner_row.astype(F32), 0.0), axis=1, keepdims=True
    ).astype(jnp.int32)
    same = owner_col == owner_row
    rank_row = jnp.sum(jnp.where(same & (k0 < k1), 1.0, 0.0), axis=0, keepdims=True).astype(jnp.int32)
    rank_col = jnp.sum(jnp.where(same & (k1 < k0), 1.0, 0.0), axis=1, keepdims=True).astype(jnp.int32)

    owners_hot = jnp.where(iota((devices, 256), 0) == owner_row, 1.0, 0.0)
    weighted = (owners_hot * (pos_row + 1).astype(F32)).astype(BF16)
    ranks_hot = hot(iota((PATCH, 256), 0) - SLOT_LANE == rank_row)
    slots = lax.dot_general(weighted, ranks_hot, NT, preferred_element_type=F32)

    coarse_copy.wait()
    cells = coarse.shape[1]
    away = (holder[0] - me) * 65536
    q = iota((cells, yw), 0)
    choose_y = hot(q == iota((cells, yw), 1) + (corner[1] - 1))
    p = iota((wrows, cells), 1) - iota((wrows, cells), 0) - (corner[0] + away)
    choose_x = jnp.concatenate([hot(p == first_parent(a * tile_x - 3)) for a in range(nx)], axis=0)
    windows = []
    for f in range(FIELDS):
        narrow = dot(coarse[f], choose_y).astype(BF16)
        windows.append(dot(choose_x, narrow))
    lane_group = iota((nx * wrows, PATCH), 1) // WCOLS
    lane = iota((wrows, PATCH), 1)
    slot_place = (iota((wrows, PATCH), 0) == 0) & (lane >= SLOT_LANE) & (lane < WCOLS)
    for b in range(ny):
        base = first_parent(b * tile_y - 3) + 1
        piece = jnp.zeros((nx * wrows, PATCH), F32)
        for f in range(FIELDS):
            moved = pltpu.roll(windows[f], (f * WCOLS - base) % yw, 1)[:, 0:PATCH]
            piece = jnp.where(lane_group == f, moved, piece)
        for a in range(nx):
            d = a * ny + b
            part = piece[a * wrows : (a + 1) * wrows]
            tx1[d] = jnp.where(slot_place, slots[d : d + 1, :], part).astype(BF16)

    pl.semaphore_wait(barrier, devices - 1)

    def send(phase, source, target):
        def one(t, carry):
            other = lax.rem(me + t, devices)
            pltpu.make_async_remote_copy(
                src_ref=source(other),
                dst_ref=target,
                send_sem=send_sem.at[phase],
                recv_sem=recv_sem.at[phase],
                device_id=(lax.div(other, ny), lax.rem(other, ny)),
                device_id_type=MESH,
            ).start()
            return carry

        lax.fori_loop(1, devices, one, 0)

    def all_of(ref, sem):
        pltpu.make_async_copy(ref, ref, sem).wait()

    def others(ref, rows):
        return ref.at[pl.ds(0, (devices - 1) * rows)]

    west, east = lax.rem(ix + nx - 1, nx), lax.rem(ix + 1, nx)
    south, north = lax.rem(iy + ny - 1, ny), lax.rem(iy + 1, ny)
    left, right = pl.ds(0, 16), pl.ds(16, 16)
    low, high = pl.ds(0, 128), pl.ds(128, 128)
    halos = [
        (centre.at[:, pl.ds(tile_x - HALO, HALO), :], rows_in.at[0], (east, iy)),
        (centre.at[:, pl.ds(0, HALO), :], rows_in.at[1], (west, iy)),
        (strips.at[right], cols_in.at[left], (ix, north)),
        (strips.at[left], cols_in.at[right], (ix, south)),
        (strips.at[right, high], corners_in.at[0, left], (east, north)),
        (strips.at[left, high], corners_in.at[0, right], (east, south)),
        (strips.at[right, low], corners_in.at[1, left], (west, north)),
        (strips.at[left, low], corners_in.at[1, right], (west, south)),
    ]
    halos = [
        pltpu.make_async_remote_copy(
            src_ref=src, dst_ref=dst, send_sem=halo_send.at[n], recv_sem=halo_recv.at[n],
            device_id=where, device_id_type=MESH,
        )
        for n, (src, dst, where) in enumerate(halos)
    ]
    for copy in halos:
        copy.start()
    send(0, lambda other: tx1.at[other], rx1.at[me])
    own1 = pltpu.make_async_copy(tx1.at[me], rx1.at[me], local_sem.at[1])
    own1.start()

    target = owner_row * jp + rank_row

    chunk = per * jp

    def dispatch_rows(c):
        start = pl.multiple_of(c * chunk, chunk)
        row = iota((chunk, 256), 0) + start
        for f in range(FIELDS):
            pmat[pl.ds(start, chunk), f * 256 : (f + 1) * 256] = hot(row == target + f * cap)

    each(devices // per, dispatch_rows)
    flux_pack[...] = jnp.zeros(flux_pack.shape, BF16)

    op_high = op[...].astype(BF16)
    op_low = (op[...] - op_high.astype(F32)).astype(BF16)
    pitch = layers * 8
    marine_rows = marine_in.reshape(MARINE * pitch, PATCH)
    mixed_rows = mixed.reshape(MARINE * pitch, PATCH)

    def mix(c):
        for n in range(4):
            fetch(4 * c + n).wait()
        for f in range(FIELDS):
            rows = [pl.ds((4 * c + n) * pitch + f, layers, stride=8) for n in range(4)]
            value = jnp.concatenate([marine_rows[at, :] for at in rows], axis=1)
            m_high = value.astype(BF16)
            m_low = (value - m_high.astype(F32)).astype(BF16)
            value = dot(op_high, m_high) + (dot(op_low, m_high) + dot(op_high, m_low))
            for n, at in enumerate(rows):
                mixed_rows[at, :] = value[:, n * PATCH : (n + 1) * PATCH]

    each(MARINE // 4, mix)
    column = jnp.broadcast_to(op[:, 0:1], (layers, PATCH))
    for f in range(8):
        op_column[pl.ds(f, layers, stride=8), :] = column
    coarse_rows[...] = jnp.zeros(coarse_rows.shape, F32)
    for g in range(MARINE):
        coarse_rows[g * 8 : g * 8 + FIELDS, :] = exchange[:, g * PATCH : (g + 1) * PATCH]

    own1.wait()
    all_of(others(rx1, 1), recv_sem.at[0])
    for copy in halos:
        copy.wait_recv()

    window = lax.fori_loop(
        0, devices, lambda s, total: total + rx1[s].astype(F32), jnp.zeros((wrows, PATCH), F32)
    ).astype(BF16)
    height = tile_x + 2 * HALO
    fx = (iota((height, wrows), 0) + (ix * tile_x - HALO)).astype(F32)
    first_x = (4 * (ix * tile_x - 3) - 11 + 26) // 26 - 1
    at_x = (fx + 0.5) * (2.0 / 13.0) - 0.5 + corner[0].astype(F32)
    px = (iota((height, wrows), 1) + (first_x + corner[0])).astype(F32)
    wx = jnp.maximum(0.0, 1.0 - jnp.abs(at_x - px)).astype(BF16)
    lane_y = iota((PATCH, PATCH), 0)
    lane_y = lane_y - jnp.where(lane_y >= PATCH - 16, PATCH, 0)
    fy = (lane_y + iy * tile_y).astype(F32)
    first_y = (4 * (iy * tile_y - 3) - 11 + 26) // 26 - 1
    at_y = (fy + 0.5) * (2.0 / 13.0) - 0.5 + corner[1].astype(F32)
    py = ((iota((PATCH, PATCH), 1) & (WCOLS - 1)) + (first_y + corner[1])).astype(F32)
    wy = jnp.maximum(0.0, 1.0 - jnp.abs(at_y - py))
    group_y = iota((PATCH, PATCH), 1) // WCOLS

    side = lax.dot_general(cols_in[...], place, TN, preferred_element_type=F32)
    side_low = lax.dot_general(corners_in[0], place, TN, preferred_element_type=F32)
    side_high = lax.dot_general(corners_in[1], place, TN, preferred_element_type=F32)

    gi = iota((height, PATCH), 0) + (ix * tile_x - HALO)
    gj = iota((height, PATCH), 1)
    gj = gj - jnp.where(gj >= PATCH - 16, PATCH, 0) + iy * tile_y
    inside = (gi >= 0) & (gi < nx * tile_x) & (gj >= 0) & (gj < ny * tile_y)
    final = []
    for f in range(FIELDS):
        wy_f = jnp.where(group_y == f, wy, 0.0).astype(BF16)
        partial = lax.dot_general(window, wy_f, NT, preferred_element_type=F32).astype(BF16)
        forcing = dot(wx, partial)
        cut = slice(f * PATCH, (f + 1) * PATCH)
        state = jnp.concatenate(
            [
                rows_in[0, f] + side_low[56:64, cut],
                centre[f] + side[0:tile_x, cut],
                rows_in[1, f] + side_high[0:8, cut],
            ],
            axis=0,
        )
        state = jnp.where(inside, state, 0.0)
        for _ in range(STEPS):
            beside = (
                pltpu.roll(state, 1, 0) + pltpu.roll(state, height - 1, 0)
                + pltpu.roll(state, 1, 1) + pltpu.roll(state, PATCH - 1, 1)
            )
            state = state + DIFFUSE * (beside - 4.0 * state) + RELAX * (forcing - state)
            state = jnp.where(inside, state, 0.0)
        state = state[HALO : HALO + tile_x]
        nest_out[f] = state[:, 0:tile_y]
        final.append(state)

    flux_tile[:, 0:tile_y] = skin[...]
    heat = flux_tile[...]
    u, v, ta, qa = final
    drag = DRAG * jnp.sqrt(1.0 + u * u + v * v)
    lane = iota((tile_x // 4, PATCH), 1)
    for f, flux in enumerate((drag * (ta - heat), drag * (qa - 0.5 * heat), drag * u, drag * v)):
        flux_tile[...] = flux
        f0, f1, f2, f3 = [flux_tile[pl.ds(n, tile_x // 4, stride=4), :] for n in range(4)]
        f1, f2 = pltpu.roll(f1, 96, 1), pltpu.roll(f2, 64, 1)
        flux_rows[pl.ds(0, blocks // 3, stride=3), :] = jnp.where(lane < 96, f0, f1)
        flux_rows[pl.ds(1, blocks // 3, stride=3), :] = jnp.where(lane < 64, f1, f2)
        flux_rows[pl.ds(2, blocks // 3, stride=3), :] = jnp.where(lane < 32, f2, pltpu.roll(f3, 32, 1))
        flux_pack[f * 256 : f * 256 + blocks, :] = flux_rows[...].astype(BF16)

    def part(ref, device, rows):
        return ref.at[pl.ds(pl.multiple_of(device * rows, 16), rows)]

    def flux_to(other):
        return pltpu.make_async_remote_copy(
            src_ref=part(tx2, other, jp),
            dst_ref=part(rx2, me, jp),
            send_sem=send_sem.at[1],
            recv_sem=recv_sem.at[1],
            device_id=(lax.div(other, ny), lax.rem(other, ny)),
            device_id_type=MESH,
        )

    def dispatch(c):
        turn = lax.rem(c + lax.div(me, per), devices // per)
        rows = pl.ds(pl.multiple_of(turn * chunk, chunk), chunk)
        tx2[rows, :] = dot(pmat[rows, :], flux_pack[...]).astype(BF16)
        for n in range(per):
            other = turn * per + n

            @pl.when(other != me)
            def _():
                flux_to(other).start()

    each(devices // per, dispatch)
    own2 = pltpu.make_async_copy(part(tx2, me, jp), part(rx2, me, jp), local_sem.at[2])
    own2.start()

    got = rx1[:, 0:16, :].astype(F32)[:, 0, :].astype(BF16)

    def spread_slots(pitch, fields):
        period = math.lcm(pitch, PATCH)
        a, b = iota((PATCH, period), 0) - SLOT_LANE, iota((PATCH, period), 1)
        rank = b - pitch * sum([jnp.where(b >= n * pitch, 1, 0) for n in range(1, period // pitch)])
        inner = sum([jnp.where(rank >= f * cap, 1, 0) for f in range(1, fields + 1)])
        tiled = dot(got, hot((a == rank - inner * cap) & (a >= 0) & (inner < fields)))
        tiled = jnp.where(tiled > 0.5, tiled * 8.0 + inner[0:1].astype(F32), 0.0)
        tiled = jnp.concatenate([tiled] * (devices * pitch // period), axis=1)
        s, l = iota(tiled.shape, 0), iota(tiled.shape, 1)
        mine = (l >= s * pitch) & (l < (s + 1) * pitch)
        return jnp.sum(jnp.where(mine, tiled, 0.0), axis=0, keepdims=True).astype(jnp.int32) - 8

    amat[...] = hot(iota((MARINE * 8, devices * jp), 0) == spread_slots(jp, FIELDS))
    count = jnp.sum(amat[...].astype(F32), axis=1, keepdims=True)
    qmat[...] = hot(iota((MARINE, devices * rp), 0) * 8 == spread_slots(rp, 1))
    least = jnp.maximum(count, 1.0)
    empty = jnp.where(count == 0.0, coarse_rows[...], 0.0)
    skin_base = mixed_rows[pl.ds(0, MARINE, stride=pitch), :]

    own2.wait()
    all_of(others(rx2, jp), recv_sem.at[1])
    forced[...] = (dot(amat[...], rx2[...]) + empty) / least
    new_skin = skin_base + op[0:1, 0:1] * forced[pl.ds(0, MARINE, stride=8), :]

    def select(matrix, value, dims):
        high = value.astype(BF16)
        low = (value - high.astype(F32)).astype(BF16)
        both = lax.dot_general(
            matrix, jnp.concatenate([high, low], axis=1), dims, preferred_element_type=F32
        )
        return both[:, 0:PATCH] + both[:, PATCH:]

    tx3[...] = select(qmat[...], new_skin, TN).reshape(tx3.shape)
    send(2, lambda other: tx3.at[other, pl.ds(0, cap)], rx3.at[me, pl.ds(0, cap)])
    own3 = pltpu.make_async_copy(tx3.at[me, pl.ds(0, cap)], rx3.at[me, pl.ds(0, cap)], local_sem.at[3])
    own3.start()

    column = op_column[...].reshape(layers, 8, PATCH)

    def force(g):
        mixed[g] = mixed[g] + column * forced[pl.ds(pl.multiple_of(g * 8, 8), 8), :][None]
        keep(g).start()

    each(MARINE, force)
    where_from = hot(iota((blocks, devices * rp), 1) == owner_col * rp + rank_col)
    for copy in halos:
        copy.wait_send()
    all_of(others(tx1, 1), send_sem.at[0])
    all_of(others(tx2, jp), send_sem.at[1])
    own3.wait()
    all_of(rx3.at[pl.ds(0, devices - 1), pl.ds(0, cap)], recv_sem.at[2])
    flux_rows[...] = select(where_from, rx3[...].reshape(devices * rp, PATCH), (((1,), (0,)), ((), ())))
    h0, h1, h2 = [flux_rows[pl.ds(n, blocks // 3, stride=3), :] for n in range(3)]
    h1 = pltpu.roll(h1, 64, 1)
    quarter = tile_x // 4
    flux_tile[pl.ds(0, quarter, stride=4), :] = h0
    flux_tile[pl.ds(1, quarter, stride=4), :] = jnp.where(
        lane < 32, pltpu.roll(h0, 32, 1), pltpu.roll(h1, 96, 1)
    )
    flux_tile[pl.ds(2, quarter, stride=4), :] = jnp.where(lane < 64, h1, pltpu.roll(h2, 64, 1))
    flux_tile[pl.ds(3, quarter, stride=4), :] = pltpu.roll(h2, 96, 1)
    heat_out[...] = flux_tile[:, 0:tile_y]
    all_of(tx3.at[pl.ds(0, devices - 1), pl.ds(0, cap)], send_sem.at[2])
    each(MARINE, lambda g: keep(g).wait())


def on_device(nx, ny, fine, skin, coarse, holder, corner, owner, position, exchange, marine, op):
    devices = nx * ny
    tile_x, tile_y = fine.shape[1:]
    blocks = tile_x * tile_y // PATCH
    cap = max(2, (2 * blocks + devices - 1) // devices)
    jp = -(-FIELDS * cap // 16) * 16
    rp = -(-cap // 16) * 16
    spans = [
        first_parent(min((a + 1) * tile_x + 2, nx * tile_x - 1)) - first_parent(a * tile_x - 3) + 2
        for a in range(nx)
    ]
    wrows = -(-max(spans) // 16) * 16
    per = 2 ** int(math.log2(256 // jp))
    last = first_parent((ny - 1) * tile_y - 3) + 1 + 18
    yw = -(-last // PATCH) * PATCH
    layers, cells = marine.shape[1:]
    vmem = pl.BlockSpec(memory_space=pltpu.VMEM)
    smem = pl.BlockSpec(memory_space=pltpu.SMEM)
    anywhere = pl.BlockSpec(memory_space=pl.ANY)
    nest, marine_new, heat = pl.pallas_call(
        functools.partial(kernel, nx, ny, cap, jp, rp, yw, wrows, per),
        out_shape=(
            jax.ShapeDtypeStruct(fine.shape, F32),
            jax.ShapeDtypeStruct((layers, FIELDS, cells), F32),
            jax.ShapeDtypeStruct(skin.shape, F32),
        ),
        in_specs=[smem, smem, vmem, vmem, vmem, vmem, anywhere, vmem, anywhere, vmem],
        out_specs=(vmem, anywhere, vmem),
        scratch_shapes=[
            pltpu.VMEM(coarse.shape, BF16),
            pltpu.VMEM((8, 256), jnp.int32),
            pltpu.VMEM((FIELDS, tile_x, PATCH), F32),
            pltpu.VMEM((32, 256), BF16),
            pltpu.VMEM((2, FIELDS, HALO, PATCH), F32),
            pltpu.VMEM((32, 256), BF16),
            pltpu.VMEM((2, 32, PATCH), BF16),
            pltpu.VMEM((devices, wrows, PATCH), BF16),
            pltpu.VMEM((devices, wrows, PATCH), BF16),
            pltpu.VMEM((devices * jp, FIELDS * 256), BF16),
            pltpu.VMEM((tile_x, PATCH), F32),
            pltpu.VMEM((blocks, PATCH), F32),
            pltpu.VMEM((FIELDS * 256, PATCH), BF16),
            pltpu.VMEM((devices * jp, PATCH), BF16),
            pltpu.VMEM((devices * jp, PATCH), BF16),
            pltpu.VMEM((MARINE * 8, devices * jp), BF16),
            pltpu.VMEM((MARINE, devices * rp), BF16),
            pltpu.VMEM((devices, rp, PATCH), F32),
            pltpu.VMEM((devices, rp, PATCH), F32),
            pltpu.VMEM((MARINE, layers, 8, PATCH), F32),
            pltpu.VMEM((MARINE, layers, 8, PATCH), F32),
            pltpu.VMEM((layers * 8, PATCH), F32),
            pltpu.VMEM((MARINE * 8, PATCH), F32),
            pltpu.VMEM((MARINE * 8, PATCH), F32),
            pltpu.SemaphoreType.DMA((MARINE,)),
            pltpu.SemaphoreType.DMA((MARINE,)),
            pltpu.SemaphoreType.DMA((4,)),
            pltpu.SemaphoreType.DMA((8,)),
            pltpu.SemaphoreType.DMA((8,)),
            pltpu.SemaphoreType.DMA((3,)),
            pltpu.SemaphoreType.DMA((3,)),
        ],
        compiler_params=pltpu.CompilerParams(
            collective_id=0, has_side_effects=True, vmem_limit_bytes=56 * 1024 * 1024
        ),
    )(
        holder, corner, owner.reshape(1, blocks), position.reshape(1, blocks),
        fine, skin, coarse, exchange, jnp.transpose(marine, (1, 0, 2)), op,
    )
    return nest, jnp.transpose(marine_new, (1, 0, 2)), heat


def solution(mesh):
    in_specs = (
        P(None, "gx", "gy"),
        P("gx", "gy"),
        P(None, "gx", "gy"),
        P(),
        P(),
        P(("gx", "gy"), None),
        P(("gx", "gy")),
        P(None, ("gx", "gy")),
        P(None, None, ("gx", "gy")),
        P(),
    )
    out_specs = (P(None, "gx", "gy"), P(None, None, ("gx", "gy")), P("gx", "gy"))
    return jax.shard_map(
        functools.partial(on_device, mesh.shape["gx"], mesh.shape["gy"]),
        mesh=mesh,
        in_specs=in_specs,
        out_specs=out_specs,
        check_vma=False,
    )
```

time: 51.7 us -> 44.9 us (0.87)
  local copies, waits for them, and re-layouts: 11.1 us -> 6.02 us
  Pallas kernels: 38.2 us -> 37.4 us
  other arithmetic: 0.7 us -> 0 us
    unnamed x20 -> x5, local copies, waits for them, and re-layouts: 9.52 us -> 6.02 us
    reshape x1 -> x0, local copies, waits for them, and re-layouts: 1.61 us -> none  [on_device(): return (nest, marine_new, heat.reshape(tile_x, tile_y))]
    pallas_call x1, Pallas kernels: 38.2 us -> 37.4 us  [on_device(): pl.pallas_call(functools.partial(kernel, nx, ny, cap, jp, rp, yw, wrows,...]
    another operation x1 -> x0, other arithmetic: 0.7 us -> none  [on_device(): jnp.stack([owner[:, 0], position])]
where the time goes in v2:
time: 44.9 us; the launch traced here: 44.7 us
  Pallas kernels  37.4 us (83%)
  local copies, waits for them, and re-layouts  6.02 us (13%)
  between operations  1.29 us (3%)
    pallas_call x1, Pallas kernels, on_device(): pl.pallas_call(functools.partial(kernel, nx, ny, cap, jp, rp, yw, wrows,...  37.4 us
    unnamed x5, local copies, waits for them, and re-layouts  6.02 us

profile of v2, /device:TPU:0, one launch (start us, length us, event | category | flops | bytes accessed | tf_op | source)
XLA Modules:
  0.0 44.7 jit_solution(10774818245084483635)
XLA Ops:
  1.3 37.4 %shard_map.121 = (f32[4,192,96]{2,1,0:T(8,128)}, f32[41,4,4096]{2,1,0:T(4,128)}, f32[192,96]{1,0:T(8,128)}) custom-call(s32[1]{0:T(128)S(6)} %copy.16.holder, s32[2]{0:T(128)} %corner.1, s32[1,144]{1,0:T(1,128)} %bitcast.6, s32[1,144]{1,0:T(1,128)} %bitcast.7, f32[4,192,96]{2,1,0:T(8,128)} %fine.1, f32[192,96]{1,0:T(8,128)} %skin.1, ...), custom_call_target="tpu_custom_call" | custom-call | tf_op jit(solution)/shard_map/pallas_call | solution.py:425
  38.7 1.8 %copy.17 = f32[4,192,96]{2,1,0:T(8,128)} copy(f32[4,192,96]{2,1,0:T(8,128)} %get-tuple-element.12) | data formatting | bytes 589824
  40.5 0.0 copy-start
  40.5 3.6 %copy.18 = f32[4,41,4096]{2,0,1:T(4,128)} copy(f32[4,41,4096]{2,0,1:T(4,128)} %bitcast.5) | data formatting | bytes 5373952
  44.1 0.0 copy-done
  44.1 0.6 %copy.19 = f32[192,96]{1,0:T(8,128)} copy(f32[192,96]{1,0:T(8,128)S(1)} %copy-done) | data formatting | bytes 147456
Async XLA Ops:
  40.5 3.6 %copy-start = (f32[192,96]{1,0:T(8,128)S(1)}, f32[192,96]{1,0:T(8,128)}, u32[]{:S(2)}) copy-start(f32[192,96]{1,0:T(8,128)} %get-tuple-element.14) | copy-start | bytes 221188

commit v3 on v2

--- a/solution.py
+++ b/solution.py
@@ -47,7 +47,7 @@
     nest_out, marine_out, heat_out,
     coarse, index_row, centre, strips, rows_in, cols_in, corners_in,
     tx1, rx1, pmat, flux_tile, flux_rows, flux_pack, tx2, rx2, amat, qmat, tx3, rx3,
-    marine_in, mixed, op_column, coarse_rows, forced,
+    marine_in, mixed, op_pad, op_column, coarse_rows, forced,
     marine_sem, out_sem, local_sem, halo_send, halo_recv, send_sem, recv_sem,
 ):
     tile_x, tile_y = fine.shape[1], fine.shape[2]
@@ -76,12 +76,12 @@
 
     def fetch(g):
         return pltpu.make_async_copy(
-            ocean_block(marine, g), marine_in.at[g, :, pl.ds(0, FIELDS), :], marine_sem.at[g]
+            ocean_block(marine, g), marine_in.at[g, pl.ds(0, layers), pl.ds(0, FIELDS), :], marine_sem.at[g]
         )
 
     def keep(g):
         return pltpu.make_async_copy(
-            mixed.at[g, :, pl.ds(0, FIELDS), :], ocean_block(marine_out, g), out_sem.at[g]
+            mixed.at[g, pl.ds(0, layers), pl.ds(0, FIELDS), :], ocean_block(marine_out, g), out_sem.at[g]
         )
 
     def each(count, work):
@@ -210,9 +210,15 @@
     each(devices // per, dispatch_rows)
     flux_pack[...] = jnp.zeros(flux_pack.shape, BF16)
 
-    op_high = op[...].astype(BF16)
-    op_low = (op[...] - op_high.astype(F32)).astype(BF16)
-    pitch = layers * 8
+    deep = marine_in.shape[1]
+    op_pad[...] = jnp.zeros(op_pad.shape, F32)
+    op_pad[0:layers, 0:layers] = op[...]
+    op_high = op_pad[...].astype(BF16).astype(F32)
+    op_low = op_pad[...] - op_high
+    op_three = op_high + pltpu.roll(op_high, deep, 1) + pltpu.roll(op_low, 2 * deep, 1)
+    op_three = op_three.astype(BF16)[:, 0 : 3 * deep]
+    pitch = deep * 8
+    marine_in[:, layers:, :, :] = jnp.zeros((MARINE, deep - layers, 8, PATCH), F32)
     marine_rows = marine_in.reshape(MARINE * pitch, PATCH)
     mixed_rows = mixed.reshape(MARINE * pitch, PATCH)
 
@@ -220,21 +226,16 @@
         for n in range(4):
             fetch(4 * c + n).wait()
         for f in range(FIELDS):
-            rows = [pl.ds((4 * c + n) * pitch + f, layers, stride=8) for n in range(4)]
+            rows = [pl.ds((4 * c + n) * pitch + f, deep, stride=8) for n in range(4)]
             value = jnp.concatenate([marine_rows[at, :] for at in rows], axis=1)
             m_high = value.astype(BF16)
             m_low = (value - m_high.astype(F32)).astype(BF16)
-            value = dot(op_high, m_high) + (dot(op_low, m_high) + dot(op_high, m_low))
+            value = dot(op_three, jnp.concatenate([m_high, m_low, m_high], axis=0))
             for n, at in enumerate(rows):
                 mixed_rows[at, :] = value[:, n * PATCH : (n + 1) * PATCH]
 
-    each(MARINE // 4, mix)
-    column = jnp.broadcast_to(op[:, 0:1], (layers, PATCH))
-    for f in range(8):
-        op_column[pl.ds(f, layers, stride=8), :] = column
-    coarse_rows[...] = jnp.zeros(coarse_rows.shape, F32)
-    for g in range(MARINE):
-        coarse_rows[g * 8 : g * 8 + FIELDS, :] = exchange[:, g * PATCH : (g + 1) * PATCH]
+    early = 3
+    each(early, mix)
 
     own1.wait()
     all_of(others(rx1, 1), recv_sem.at[0])
@@ -349,6 +350,13 @@
         mine = (l >= s * pitch) & (l < (s + 1) * pitch)
         return jnp.sum(jnp.where(mine, tiled, 0.0), axis=0, keepdims=True).astype(jnp.int32) - 8
 
+    each(MARINE // 4 - early, lambda c: mix(c + early))
+    column = jnp.broadcast_to(op[:, 0:1], (layers, PATCH))
+    for f in range(8):
+        op_column[pl.ds(f, layers, stride=8), :] = column
+    coarse_rows[...] = jnp.zeros(coarse_rows.shape, F32)
+    for g in range(MARINE):
+        coarse_rows[g * 8 : g * 8 + FIELDS, :] = exchange[:, g * PATCH : (g + 1) * PATCH]
     amat[...] = hot(iota((MARINE * 8, devices * jp), 0) == spread_slots(jp, FIELDS))
     count = jnp.sum(amat[...].astype(F32), axis=1, keepdims=True)
     qmat[...] = hot(iota((MARINE, devices * rp), 0) * 8 == spread_slots(rp, 1))
@@ -377,7 +385,7 @@
     column = op_column[...].reshape(layers, 8, PATCH)
 
     def force(g):
-        mixed[g] = mixed[g] + column * forced[pl.ds(pl.multiple_of(g * 8, 8), 8), :][None]
+        mixed[g, 0:layers] = mixed[g, 0:layers] + column * forced[pl.ds(pl.multiple_of(g * 8, 8), 8), :][None]
         keep(g).start()
 
     each(MARINE, force)
@@ -419,6 +427,7 @@
     last = first_parent((ny - 1) * tile_y - 3) + 1 + 18
     yw = -(-last // PATCH) * PATCH
     layers, cells = marine.shape[1:]
+    deep = -(-layers // 16) * 16
     vmem = pl.BlockSpec(memory_space=pltpu.VMEM)
     smem = pl.BlockSpec(memory_space=pltpu.SMEM)
     anywhere = pl.BlockSpec(memory_space=pl.ANY)
@@ -451,8 +460,9 @@
             pltpu.VMEM((MARINE, devices * rp), BF16),
             pltpu.VMEM((devices, rp, PATCH), F32),
             pltpu.VMEM((devices, rp, PATCH), F32),
-            pltpu.VMEM((MARINE, layers, 8, PATCH), F32),
-            pltpu.VMEM((MARINE, layers, 8, PATCH), F32),
+            pltpu.VMEM((MARINE, deep, 8, PATCH), F32),
+            pltpu.VMEM((MARINE, deep, 8, PATCH), F32),
+            pltpu.VMEM((deep, 256), F32),
             pltpu.VMEM((layers * 8, PATCH), F32),
             pltpu.VMEM((MARINE * 8, PATCH), F32),
             pltpu.VMEM((MARINE * 8, PATCH), F32),
@@ -465,7 +475,7 @@
             pltpu.SemaphoreType.DMA((3,)),
         ],
         compiler_params=pltpu.CompilerParams(
-            collective_id=0, has_side_effects=True, vmem_limit_bytes=56 * 1024 * 1024
+            collective_id=0, has_side_effects=True, vmem_limit_bytes=32 * 1024 * 1024
         ),
     )(
         holder, corner, owner.reshape(1, blocks), position.reshape(1, blocks),

time: 44.9 us -> 49.3 us (1.098)
  local copies, waits for them, and re-layouts: 6.02 us -> 11.4 us
  Pallas kernels: 37.4 us -> 36.2 us
    unnamed x5 -> x21, local copies, waits for them, and re-layouts: 6.02 us -> 11.4 us
    pallas_call x1, Pallas kernels: 37.4 us -> 36.2 us  [on_device(): pl.pallas_call(functools.partial(kernel, nx, ny, cap, jp, rp, yw, wrows,...]
where the time goes in v3:
time: 49.3 us; the launch traced here: 48.9 us
  Pallas kernels  36.2 us (73%)
  local copies, waits for them, and re-layouts  11.4 us (23%)
  between operations  1.3 us (3%)
    pallas_call x1, Pallas kernels, on_device(): pl.pallas_call(functools.partial(kernel, nx, ny, cap, jp, rp, yw, wrows,...  36.2 us
    unnamed x21, local copies, waits for them, and re-layouts  11.4 us

profile of v3, /device:TPU:0, one launch (start us, length us, event | category | flops | bytes accessed | tf_op | source)
XLA Modules:
  0.0 48.9 jit_solution(9431877513550111526)
XLA Ops:
  1.3 0.0 copy-start
  1.3 1.7 %copy-done = f32[4,41,4096]{2,0,1:T(4,128)S(1)} copy-done((f32[4,41,4096]{2,0,1:T(4,128)S(1)}, f32[4,41,4096]{2,0,1:T(4,128)}, u32[]{:S(2)}) %copy-start) | copy-done | bytes 2687000
  3.0 0.0 copy-start.1
  3.0 1.3 %copy-done.1 = bf16[4,384,384]{2,1,0:T(8,128)(2,1)S(1)} copy-done((bf16[4,384,384]{2,1,0:T(8,128)(2,1)S(1)}, bf16[4,384,384]{2,1,0:T(8,128)(2,1)}, u32[]{:S(2)}) %copy-start.1) | copy-done | bytes 1179672
  4.3 0.0 copy-start.2
  4.3 1.0 %copy-done.2 = f32[4,192,96]{2,1,0:T(8,128)S(1)} copy-done((f32[4,192,96]{2,1,0:T(8,128)S(1)}, f32[4,192,96]{2,1,0:T(8,128)}, u32[]{:S(2)}) %copy-start.2) | copy-done | bytes 294936
  5.3 0.0 copy-start.3
  5.3 0.9 %copy-done.3 = f32[192,96]{1,0:T(8,128)S(1)} copy-done((f32[192,96]{1,0:T(8,128)S(1)}, f32[192,96]{1,0:T(8,128)}, u32[]{:S(2)}) %copy-start.3) | copy-done | bytes 73752
  6.2 0.0 copy-start.4
  6.2 0.8 %copy-done.4 = f32[4,4096]{1,0:T(4,128)S(1)} copy-done((f32[4,4096]{1,0:T(4,128)S(1)}, f32[4,4096]{1,0:T(4,128)}, u32[]{:S(2)}) %copy-start.4) | copy-done | bytes 65560
  7.0 0.0 copy-start.5
  7.0 0.7 %copy-done.5 = f32[41,41]{1,0:T(8,128)S(1)} copy-done((f32[41,41]{1,0:T(8,128)S(1)}, f32[41,41]{1,0:T(8,128)}, u32[]{:S(2)}) %copy-start.5) | copy-done | bytes 6748
  7.8 0.0 copy-start.6
  7.8 0.7 %copy-done.6 = s32[144,1]{0,1:T(1,128)S(1)} copy-done((s32[144,1]{0,1:T(1,128)S(1)}, s32[144,1]{0,1:T(1,128)}, u32[]{:S(2)}) %copy-start.6) | copy-done | bytes 600
  8.5 0.0 copy-start.7
  8.5 0.7 %copy-done.7 = s32[144]{0:T(256)S(1)} copy-done((s32[144]{0:T(256)S(1)}, s32[144]{0:T(256)}, u32[]{:S(2)}) %copy-start.7) | copy-done | bytes 600
  9.1 0.0 copy-start.8
  9.1 0.7 %copy-done.8 = s32[2]{0:T(128)S(1)} copy-done((s32[2]{0:T(128)S(1)}, s32[2]{0:T(128)}, u32[]{:S(2)}) %copy-start.8) | copy-done | bytes 32
  9.8 36.2 %shard_map.121 = (f32[4,192,96]{2,1,0:T(8,128)S(1)}, f32[41,4,4096]{2,1,0:T(4,128)S(1)}, f32[192,96]{1,0:T(8,128)S(1)}) custom-call(s32[1]{0:T(128)S(6)} %copy.16.holder, s32[2]{0:T(128)S(1)} %copy-done.8, s32[1,144]{1,0:T(1,128)S(1)} %bitcast.6, s32[1,144]{1,0:T(1,128)S(1)} %bitcast.7, f32[4,192,96]{2,1,0:T(8,128)S(1)} %copy-done.2, ...), custom_call_target="tpu_custom_call" | custom-call | tf_op jit(solution)/shard_map/pallas_call | solution.py:434
  46.0 0.7 %copy.17 = f32[4,192,96]{2,1,0:T(8,128)} copy(f32[4,192,96]{2,1,0:T(8,128)S(1)} %get-tuple-element.12) | data formatting | bytes 589824
  46.8 1.5 %copy.18 = f32[4,41,4096]{2,0,1:T(4,128)} copy(f32[4,41,4096]{2,0,1:T(4,128)S(1)} %bitcast.5) | data formatting | bytes 5373952
  48.3 0.6 %copy.19 = f32[192,96]{1,0:T(8,128)} copy(f32[192,96]{1,0:T(8,128)S(1)} %get-tuple-element.14) | data formatting | bytes 147456
Async XLA Ops:
  1.3 1.8 %copy-start = (f32[4,41,4096]{2,0,1:T(4,128)S(1)}, f32[4,41,4096]{2,0,1:T(4,128)}, u32[]{:S(2)}) copy-start(f32[4,41,4096]{2,0,1:T(4,128)} %param.18) | copy-start | bytes 8060932
  3.0 1.3 %copy-start.1 = (bf16[4,384,384]{2,1,0:T(8,128)(2,1)S(1)}, bf16[4,384,384]{2,1,0:T(8,128)(2,1)}, u32[]{:S(2)}) copy-start(bf16[4,384,384]{2,1,0:T(8,128)(2,1)} %coarse_far.1) | copy-start | bytes 3538948
  4.3 1.0 %copy-start.2 = (f32[4,192,96]{2,1,0:T(8,128)S(1)}, f32[4,192,96]{2,1,0:T(8,128)}, u32[]{:S(2)}) copy-start(f32[4,192,96]{2,1,0:T(8,128)} %fine.1) | copy-start | bytes 884740
  5.3 0.9 %copy-start.3 = (f32[192,96]{1,0:T(8,128)S(1)}, f32[192,96]{1,0:T(8,128)}, u32[]{:S(2)}) copy-start(f32[192,96]{1,0:T(8,128)} %skin.1) | copy-start | bytes 221188
  6.2 0.8 %copy-start.4 = (f32[4,4096]{1,0:T(4,128)S(1)}, f32[4,4096]{1,0:T(4,128)}, u32[]{:S(2)}) copy-start(f32[4,4096]{1,0:T(4,128)} %exchange.1) | copy-start | bytes 196612
  7.0 0.7 %copy-start.5 = (f32[41,41]{1,0:T(8,128)S(1)}, f32[41,41]{1,0:T(8,128)}, u32[]{:S(2)}) copy-start(f32[41,41]{1,0:T(8,128)} %op.1) | copy-start | bytes 20176
  7.8 0.7 %copy-start.6 = (s32[144,1]{0,1:T(1,128)S(1)}, s32[144,1]{0,1:T(1,128)}, u32[]{:S(2)}) copy-start(s32[144,1]{0,1:T(1,128)} %param.15) | copy-start | bytes 1732
  8.5 0.7 %copy-start.7 = (s32[144]{0:T(256)S(1)}, s32[144]{0:T(256)}, u32[]{:S(2)}) copy-start(s32[144]{0:T(256)} %param.16) | copy-start | bytes 1732
  9.1 0.7 %copy-start.8 = (s32[2]{0:T(128)S(1)}, s32[2]{0:T(128)}, u32[]{:S(2)}) copy-start(s32[2]{0:T(128)} %corner.1) | copy-start | bytes 28

commit v4 on v3

--- a/solution.py
+++ b/solution.py
@@ -43,12 +43,12 @@
 
 def kernel(
     nx, ny, cap, jp, rp, yw, wrows, per,
-    holder, corner, owner, position, fine, skin, coarse_far, exchange, marine, op,
-    nest_out, marine_out, heat_out,
-    coarse, index_row, centre, strips, rows_in, cols_in, corners_in,
+    holder, corner, owner, position, fine_far, skin_far, coarse_far, exchange_far, marine, op_far,
+    nest_out, marine_out, forced_out, heat_out,
+    fine, skin, coarse, exchange, op, nest, index_row, centre, strips, rows_in, cols_in, corners_in,
     tx1, rx1, pmat, flux_tile, flux_rows, flux_pack, tx2, rx2, amat, qmat, tx3, rx3,
-    marine_in, mixed, op_pad, op_column, coarse_rows, forced,
-    marine_sem, out_sem, local_sem, halo_send, halo_recv, send_sem, recv_sem,
+    marine_in, mixed, op_pad, coarse_rows, forced,
+    in_sem, marine_sem, out_sem, nest_sem, local_sem, halo_send, halo_recv, send_sem, recv_sem,
 ):
     tile_x, tile_y = fine.shape[1], fine.shape[2]
     blocks = owner.shape[1]
@@ -57,32 +57,11 @@
     ix, iy = lax.axis_index("gx"), lax.axis_index("gy")
     me = ix * ny + iy
 
-    coarse_copy = pltpu.make_async_copy(coarse_far, coarse, local_sem.at[0])
-    coarse_copy.start()
-    rx3[...] = jnp.zeros(rx3.shape, F32)
-    barrier = pltpu.get_barrier_semaphore()
-
-    def greet(t, carry):
-        other = lax.rem(me + t, devices)
-        pl.semaphore_signal(
-            barrier, inc=1, device_id=(lax.div(other, ny), lax.rem(other, ny)), device_id_type=MESH
-        )
-        return carry
-
-    lax.fori_loop(1, devices, greet, 0)
-
-    def ocean_block(ref, g):
-        return ref.at[:, :, pl.ds(pl.multiple_of(g * PATCH, PATCH), PATCH)]
-
-    def fetch(g):
-        return pltpu.make_async_copy(
-            ocean_block(marine, g), marine_in.at[g, pl.ds(0, layers), pl.ds(0, FIELDS), :], marine_sem.at[g]
-        )
-
-    def keep(g):
-        return pltpu.make_async_copy(
-            mixed.at[g, pl.ds(0, layers), pl.ds(0, FIELDS), :], ocean_block(marine_out, g), out_sem.at[g]
-        )
+    arrays = [(coarse_far, coarse), (fine_far, fine), (skin_far, skin), (exchange_far, exchange), (op_far, op)]
+    arrays = [pltpu.make_async_copy(far, near, in_sem.at[n]) for n, (far, near) in enumerate(arrays)]
+    for copy in arrays:
+        copy.start()
+    coarse_copy, fine_copy, skin_copy, exchange_copy, op_copy = arrays
 
     def each(count, work):
         def one(n, carry):
@@ -91,8 +70,48 @@
 
         lax.fori_loop(0, count, one, 0)
 
+    power = devices & (devices - 1) == 0 and ny & (ny - 1) == 0 and devices >= 8
+
+    def place_of(device):
+        if power:
+            return (device >> (ny.bit_length() - 1), device & (ny - 1))
+        return (lax.div(device, ny), lax.rem(device, ny))
+
+    def to_others(work):
+        if not power:
+            each(devices - 1, lambda n: work(lax.rem(me + 1 + n, devices)))
+            return
+        half = devices // 2
+
+        def far(n, bit):
+            return me ^ (((n >> 2) << 3) | bit | (n & 3))
+
+        each(half, lambda n: work(far(n, 4)))
+        each(half - 1, lambda n: work(far(n + 1, 0)))
+
+    rx3[...] = jnp.zeros(rx3.shape, F32)
+    barrier = pltpu.get_barrier_semaphore()
+    to_others(
+        lambda other: pl.semaphore_signal(
+            barrier, inc=1, device_id=place_of(other), device_id_type=MESH
+        )
+    )
+    def ocean_block(ref, g):
+        return ref.at[:, :, pl.ds(pl.multiple_of(g * PATCH, PATCH), PATCH)]
+
+    def fetch(g):
+        return pltpu.make_async_copy(
+            ocean_block(marine, g), marine_in.at[g, pl.ds(0, layers), pl.ds(0, FIELDS), :], marine_sem.at[g]
+        )
+
+    def keep(g):
+        return pltpu.make_async_copy(
+            mixed.at[g, pl.ds(0, layers), pl.ds(0, FIELDS), :], ocean_block(marine_out, g), out_sem.at[g]
+        )
+
     each(MARINE, lambda g: fetch(g).start())
 
+    fine_copy.wait()
     for f in range(FIELDS):
         centre[f, :, :] = jnp.zeros((tile_x, PATCH), F32)
         centre[f, :, 0:tile_y] = fine[f]
@@ -150,19 +169,16 @@
     pl.semaphore_wait(barrier, devices - 1)
 
     def send(phase, source, target):
-        def one(t, carry):
-            other = lax.rem(me + t, devices)
-            pltpu.make_async_remote_copy(
+        to_others(
+            lambda other: pltpu.make_async_remote_copy(
                 src_ref=source(other),
                 dst_ref=target,
                 send_sem=send_sem.at[phase],
                 recv_sem=recv_sem.at[phase],
-                device_id=(lax.div(other, ny), lax.rem(other, ny)),
+                device_id=place_of(other),
                 device_id_type=MESH,
             ).start()
-            return carry
-
-        lax.fori_loop(1, devices, one, 0)
+        )
 
     def all_of(ref, sem):
         pltpu.make_async_copy(ref, ref, sem).wait()
@@ -211,6 +227,7 @@
     flux_pack[...] = jnp.zeros(flux_pack.shape, BF16)
 
     deep = marine_in.shape[1]
+    op_copy.wait()
     op_pad[...] = jnp.zeros(op_pad.shape, F32)
     op_pad[0:layers, 0:layers] = op[...]
     op_high = op_pad[...].astype(BF16).astype(F32)
@@ -233,6 +250,8 @@
             value = dot(op_three, jnp.concatenate([m_high, m_low, m_high], axis=0))
             for n, at in enumerate(rows):
                 mixed_rows[at, :] = value[:, n * PATCH : (n + 1) * PATCH]
+        for n in range(4):
+            keep(4 * c + n).start()
 
     early = 3
     each(early, mix)
@@ -291,9 +310,12 @@
             state = state + DIFFUSE * (beside - 4.0 * state) + RELAX * (forcing - state)
             state = jnp.where(inside, state, 0.0)
         state = state[HALO : HALO + tile_x]
-        nest_out[f] = state[:, 0:tile_y]
+        nest[f] = state
         final.append(state)
 
+    nest_copy = pltpu.make_async_copy(nest, nest_out, nest_sem)
+    nest_copy.start()
+    skin_copy.wait()
     flux_tile[:, 0:tile_y] = skin[...]
     heat = flux_tile[...]
     u, v, ta, qa = final
@@ -317,12 +339,19 @@
             dst_ref=part(rx2, me, jp),
             send_sem=send_sem.at[1],
             recv_sem=recv_sem.at[1],
-            device_id=(lax.div(other, ny), lax.rem(other, ny)),
+            device_id=place_of(other),
             device_id_type=MESH,
         )
 
+    turns = devices // per
+
     def dispatch(c):
-        turn = lax.rem(c + lax.div(me, per), devices // per)
+        if power:
+            half = turns // 2
+            late = jnp.where(c >= half, 1, 0)
+            turn = (((c - late * half) << 1) | (1 - late)) ^ (me >> (per.bit_length() - 1))
+        else:
+            turn = lax.rem(c + lax.div(me, per), turns)
         rows = pl.ds(pl.multiple_of(turn * chunk, chunk), chunk)
         tx2[rows, :] = dot(pmat[rows, :], flux_pack[...]).astype(BF16)
         for n in range(per):
@@ -332,7 +361,7 @@
             def _():
                 flux_to(other).start()
 
-    each(devices // per, dispatch)
+    each(turns, dispatch)
     own2 = pltpu.make_async_copy(part(tx2, me, jp), part(rx2, me, jp), local_sem.at[2])
     own2.start()
 
@@ -351,9 +380,7 @@
         return jnp.sum(jnp.where(mine, tiled, 0.0), axis=0, keepdims=True).astype(jnp.int32) - 8
 
     each(MARINE // 4 - early, lambda c: mix(c + early))
-    column = jnp.broadcast_to(op[:, 0:1], (layers, PATCH))
-    for f in range(8):
-        op_column[pl.ds(f, layers, stride=8), :] = column
+    exchange_copy.wait()
     coarse_rows[...] = jnp.zeros(coarse_rows.shape, F32)
     for g in range(MARINE):
         coarse_rows[g * 8 : g * 8 + FIELDS, :] = exchange[:, g * PATCH : (g + 1) * PATCH]
@@ -382,13 +409,8 @@
     own3 = pltpu.make_async_copy(tx3.at[me, pl.ds(0, cap)], rx3.at[me, pl.ds(0, cap)], local_sem.at[3])
     own3.start()
 
-    column = op_column[...].reshape(layers, 8, PATCH)
-
-    def force(g):
-        mixed[g, 0:layers] = mixed[g, 0:layers] + column * forced[pl.ds(pl.multiple_of(g * 8, 8), 8), :][None]
-        keep(g).start()
-
-    each(MARINE, force)
+    for g in range(MARINE):
+        forced_out[:, g * PATCH : (g + 1) * PATCH] = forced[g * 8 : g * 8 + FIELDS, :]
     where_from = hot(iota((blocks, devices * rp), 1) == owner_col * rp + rank_col)
     for copy in halos:
         copy.wait_send()
@@ -406,7 +428,8 @@
     )
     flux_tile[pl.ds(2, quarter, stride=4), :] = jnp.where(lane < 64, h1, pltpu.roll(h2, 64, 1))
     flux_tile[pl.ds(3, quarter, stride=4), :] = pltpu.roll(h2, 96, 1)
-    heat_out[...] = flux_tile[:, 0:tile_y]
+    heat_out[...] = flux_tile[...]
+    nest_copy.wait()
     all_of(tx3.at[pl.ds(0, devices - 1), pl.ds(0, cap)], send_sem.at[2])
     each(MARINE, lambda g: keep(g).wait())
 
@@ -431,17 +454,23 @@
     vmem = pl.BlockSpec(memory_space=pltpu.VMEM)
     smem = pl.BlockSpec(memory_space=pltpu.SMEM)
     anywhere = pl.BlockSpec(memory_space=pl.ANY)
-    nest, marine_new, heat = pl.pallas_call(
+    nest, mixed, forced, heat = pl.pallas_call(
         functools.partial(kernel, nx, ny, cap, jp, rp, yw, wrows, per),
         out_shape=(
-            jax.ShapeDtypeStruct(fine.shape, F32),
+            jax.ShapeDtypeStruct((FIELDS, tile_x, PATCH), F32),
             jax.ShapeDtypeStruct((layers, FIELDS, cells), F32),
-            jax.ShapeDtypeStruct(skin.shape, F32),
+            jax.ShapeDtypeStruct((FIELDS, cells), F32),
+            jax.ShapeDtypeStruct((tile_x, PATCH), F32),
         ),
-        in_specs=[smem, smem, vmem, vmem, vmem, vmem, anywhere, vmem, anywhere, vmem],
-        out_specs=(vmem, anywhere, vmem),
+        in_specs=[smem, smem, vmem, vmem] + [anywhere] * 6,
+        out_specs=(anywhere, anywhere, vmem, vmem),
         scratch_shapes=[
+            pltpu.VMEM(fine.shape, F32),
+            pltpu.VMEM(skin.shape, F32),
             pltpu.VMEM(coarse.shape, BF16),
+            pltpu.VMEM(exchange.shape, F32),
+            pltpu.VMEM(op.shape, F32),
+            pltpu.VMEM((FIELDS, tile_x, PATCH), F32),
             pltpu.VMEM((8, 256), jnp.int32),
             pltpu.VMEM((FIELDS, tile_x, PATCH), F32),
             pltpu.VMEM((32, 256), BF16),
@@ -463,11 +492,12 @@
             pltpu.VMEM((MARINE, deep, 8, PATCH), F32),
             pltpu.VMEM((MARINE, deep, 8, PATCH), F32),
             pltpu.VMEM((deep, 256), F32),
-            pltpu.VMEM((layers * 8, PATCH), F32),
             pltpu.VMEM((MARINE * 8, PATCH), F32),
             pltpu.VMEM((MARINE * 8, PATCH), F32),
+            pltpu.SemaphoreType.DMA((5,)),
             pltpu.SemaphoreType.DMA((MARINE,)),
             pltpu.SemaphoreType.DMA((MARINE,)),
+            pltpu.SemaphoreType.DMA,
             pltpu.SemaphoreType.DMA((4,)),
             pltpu.SemaphoreType.DMA((8,)),
             pltpu.SemaphoreType.DMA((8,)),
@@ -475,13 +505,14 @@
             pltpu.SemaphoreType.DMA((3,)),
         ],
         compiler_params=pltpu.CompilerParams(
-            collective_id=0, has_side_effects=True, vmem_limit_bytes=32 * 1024 * 1024
+            collective_id=0, has_side_effects=True, vmem_limit_bytes=56 * 1024 * 1024
         ),
     )(
         holder, corner, owner.reshape(1, blocks), position.reshape(1, blocks),
         fine, skin, coarse, exchange, jnp.transpose(marine, (1, 0, 2)), op,
     )
-    return nest, jnp.transpose(marine_new, (1, 0, 2)), heat
+    marine_new = mixed + op[:, 0][:, None, None] * forced[None]
+    return nest[:, :, 0:tile_y], jnp.transpose(marine_new, (1, 0, 2)), heat[:, 0:tile_y]
 
 
 def solution(mesh):

time: 49.3 us -> 45.3 us (0.919)
  local copies, waits for them, and re-layouts: 11.4 us -> 2.24 us
  other arithmetic: 0 us -> 4.36 us
  Pallas kernels: 36.2 us -> 37.2 us
    unnamed x21 -> x6, local copies, waits for them, and re-layouts: 11.4 us -> 1.39 us
    transpose x0 -> x1, other arithmetic: none -> 4.36 us  [on_device(): jnp.transpose(marine_new, (1, 0, 2))]
    pallas_call x1, Pallas kernels: 36.2 us -> 37.2 us  [on_device(): pl.pallas_call(functools.partial(kernel, nx, ny, cap, jp, rp, yw, wrows,...]
    slice x0 -> x1, local copies, waits for them, and re-layouts: none -> 0.85 us  [on_device(): marine_new = mixed + op[:, 0][:, None, None] * forced[None]]
where the time goes in v4:
time: 45.3 us; the launch traced here: 45.1 us
  Pallas kernels  37.2 us (82%)
  other arithmetic  4.36 us (10%)
  local copies, waits for them, and re-layouts  2.24 us (5%)
  between operations  1.3 us (3%)
    pallas_call x1, Pallas kernels, on_device(): pl.pallas_call(functools.partial(kernel, nx, ny, cap, jp, rp, yw, wrows,...  37.2 us
    transpose x1, other arithmetic, on_device(): jnp.transpose(marine_new, (1, 0, 2))  4.36 us
    unnamed x6, local copies, waits for them, and re-layouts  1.39 us

profile of v4, /device:TPU:0, one launch (start us, length us, event | category | flops | bytes accessed | tf_op | source)
XLA Modules:
  0.0 45.1 jit_solution(18042020156669400699)
XLA Ops:
  1.3 0.8 %slice_reduce_fusion = f32[41]{0:T(128)S(1)} fusion(f32[41,41]{1,0:T(8,128)} %op_far.1), kind=kLoop, calls=%fused_computation.1 | loop fusion | bytes 328 | tf_op jit(solution)/shard_map/slice | solution.py:514
  2.1 37.2 %shard_map.121 = (f32[4,192,128]{2,1,0:T(8,128)}, f32[41,4,4096]{2,1,0:T(4,128)}, f32[4,4096]{1,0:T(4,128)}, f32[192,128]{1,0:T(8,128)}) custom-call(s32[1]{0:T(128)S(6)} %copy.15.holder, s32[2]{0:T(128)} %corner.1, s32[1,144]{1,0:T(1,128)} %bitcast.10, s32[1,144]{1,0:T(1,128)} %bitcast.11, f32[4,192,96]{2,1,0:T(8,128)} %fine_far.1, f32[192,96]{1,0:T(8,128)} %skin_far.1, ...), custom_call_target="tpu_custom_call" | custom-call | tf_op jit(solution)/shard_map/pallas_call | solution.py:457
  39.3 0.0 copy-start
  39.3 0.0 copy-start.1
  39.4 4.4 %add_bitcast_fusion = f32[4,41,4096]{2,0,1:T(4,128)} fusion(f32[41,4,4096]{2,1,0:T(4,128)} %get-tuple-element.8, f32[4,4096]{1,0:T(4,128)} %get-tuple-element.9, f32[41]{0:T(128)S(1)} %slice_reduce_fusion), kind=kLoop, calls=%fused_computation | loop fusion | flops 1343488 | bytes 5439652 | tf_op jit(solution)/shard_map/transpose | solution.py:515
  43.7 0.0 copy-done
  43.7 0.7 %copy.16 = f32[4,192,96]{2,1,0:T(8,128)} copy(f32[4,192,96]{2,1,0:T(8,128)S(1)} %bitcast.8) | data formatting | bytes 589824
  44.5 0.0 copy-done.1
  44.5 0.6 %copy.17 = f32[192,96]{1,0:T(8,128)} copy(f32[192,96]{1,0:T(8,128)S(1)} %bitcast.9) | data formatting | bytes 147456
Async XLA Ops:
  39.3 4.4 %copy-start = (f32[4,192,128]{2,1,0:T(8,128)S(1)}, f32[4,192,128]{2,1,0:T(8,128)}, u32[]{:S(2)}) copy-start(f32[4,192,128]{2,1,0:T(8,128)} %get-tuple-element.7) | copy-start | bytes 1179652
  39.3 5.1 %copy-start.1 = (f32[192,128]{1,0:T(8,128)S(1)}, f32[192,128]{1,0:T(8,128)}, u32[]{:S(2)}) copy-start(f32[192,128]{1,0:T(8,128)} %get-tuple-element.10) | copy-start | bytes 294916

commit v5 on v4

--- a/solution.py
+++ b/solution.py
@@ -81,13 +81,11 @@
         if not power:
             each(devices - 1, lambda n: work(lax.rem(me + 1 + n, devices)))
             return
-        half = devices // 2
-
-        def far(n, bit):
-            return me ^ (((n >> 2) << 3) | bit | (n & 3))
-
-        each(half, lambda n: work(far(n, 4)))
-        each(half - 1, lambda n: work(far(n + 1, 0)))
+
+        def nth(n):
+            return me ^ (((n & 1) << 2) | ((n >> 1) & 3) | ((n >> 3) << 3))
+
+        each(devices - 1, lambda n: work(nth(n + 1)))
 
     rx3[...] = jnp.zeros(rx3.shape, F32)
     barrier = pltpu.get_barrier_semaphore()
@@ -310,7 +308,7 @@
             state = state + DIFFUSE * (beside - 4.0 * state) + RELAX * (forcing - state)
             state = jnp.where(inside, state, 0.0)
         state = state[HALO : HALO + tile_x]
-        nest[f] = state
+        nest[f] = state[:, 0:tile_y]
         final.append(state)
 
     nest_copy = pltpu.make_async_copy(nest, nest_out, nest_sem)
@@ -347,9 +345,7 @@
 
     def dispatch(c):
         if power:
-            half = turns // 2
-            late = jnp.where(c >= half, 1, 0)
-            turn = (((c - late * half) << 1) | (1 - late)) ^ (me >> (per.bit_length() - 1))
+            turn = ((c + 1) & (turns - 1)) ^ (me >> (per.bit_length() - 1))
         else:
             turn = lax.rem(c + lax.div(me, per), turns)
         rows = pl.ds(pl.multiple_of(turn * chunk, chunk), chunk)
@@ -428,10 +424,44 @@
     )
     flux_tile[pl.ds(2, quarter, stride=4), :] = jnp.where(lane < 64, h1, pltpu.roll(h2, 64, 1))
     flux_tile[pl.ds(3, quarter, stride=4), :] = pltpu.roll(h2, 96, 1)
-    heat_out[...] = flux_tile[...]
+    heat_out[...] = flux_tile[:, 0:tile_y]
     nest_copy.wait()
     all_of(tx3.at[pl.ds(0, devices - 1), pl.ds(0, cap)], send_sem.at[2])
     each(MARINE, lambda g: keep(g).wait())
+
+
+def finish(
+    parts,
+    nest, mixed, forced, heat, op, nest_out, marine_out, heat_out,
+    nest_near, marine_near, forced_near, heat_near, op_near,
+    in_sem, out_sem, part_in, part_out,
+):
+    pairs = [(forced, forced_near), (op, op_near), (nest, nest_near), (heat, heat_near)]
+    copies = [pltpu.make_async_copy(far, near, in_sem.at[n]) for n, (far, near) in enumerate(pairs)]
+    width = marine_near.shape[3]
+    cuts = [pl.ds(n * width, width) for n in range(parts)]
+    fetches = [
+        pltpu.make_async_copy(mixed.at[:, :, cut], marine_near.at[n], part_in.at[n])
+        for n, cut in enumerate(cuts)
+    ]
+    for copy in copies[:2] + fetches + copies[2:]:
+        copy.start()
+    copies[0].wait()
+    copies[1].wait()
+    stores = []
+    for n, cut in enumerate(cuts):
+        fetches[n].wait()
+        push = forced_near[:, cut]
+        for layer in range(op.shape[0]):
+            marine_near[n, layer] = marine_near[n, layer] + op_near[layer : layer + 1, 0:1] * push
+        stores.append(pltpu.make_async_copy(marine_near.at[n], marine_out.at[:, :, cut], part_out.at[n]))
+        stores[-1].start()
+    for n, (near, far) in enumerate([(nest_near, nest_out), (heat_near, heat_out)]):
+        copies[2 + n].wait()
+        stores.append(pltpu.make_async_copy(near, far, out_sem.at[n]))
+        stores[-1].start()
+    for copy in stores:
+        copy.wait()
 
 
 def on_device(nx, ny, fine, skin, coarse, holder, corner, owner, position, exchange, marine, op):
@@ -457,10 +487,10 @@
     nest, mixed, forced, heat = pl.pallas_call(
         functools.partial(kernel, nx, ny, cap, jp, rp, yw, wrows, per),
         out_shape=(
-            jax.ShapeDtypeStruct((FIELDS, tile_x, PATCH), F32),
+            jax.ShapeDtypeStruct(fine.shape, F32),
             jax.ShapeDtypeStruct((layers, FIELDS, cells), F32),
             jax.ShapeDtypeStruct((FIELDS, cells), F32),
-            jax.ShapeDtypeStruct((tile_x, PATCH), F32),
+            jax.ShapeDtypeStruct(skin.shape, F32),
         ),
         in_specs=[smem, smem, vmem, vmem] + [anywhere] * 6,
         out_specs=(anywhere, anywhere, vmem, vmem),
@@ -470,7 +500,7 @@
             pltpu.VMEM(coarse.shape, BF16),
             pltpu.VMEM(exchange.shape, F32),
             pltpu.VMEM(op.shape, F32),
-            pltpu.VMEM((FIELDS, tile_x, PATCH), F32),
+            pltpu.VMEM(fine.shape, F32),
             pltpu.VMEM((8, 256), jnp.int32),
             pltpu.VMEM((FIELDS, tile_x, PATCH), F32),
             pltpu.VMEM((32, 256), BF16),
@@ -511,8 +541,30 @@
         holder, corner, owner.reshape(1, blocks), position.reshape(1, blocks),
         fine, skin, coarse, exchange, jnp.transpose(marine, (1, 0, 2)), op,
     )
-    marine_new = mixed + op[:, 0][:, None, None] * forced[None]
-    return nest[:, :, 0:tile_y], jnp.transpose(marine_new, (1, 0, 2)), heat[:, 0:tile_y]
+    parts = 8
+    nest, marine_new, heat = pl.pallas_call(
+        functools.partial(finish, parts),
+        out_shape=(
+            jax.ShapeDtypeStruct(fine.shape, F32),
+            jax.ShapeDtypeStruct((layers, FIELDS, cells), F32),
+            jax.ShapeDtypeStruct(skin.shape, F32),
+        ),
+        in_specs=[anywhere] * 5,
+        out_specs=(anywhere,) * 3,
+        scratch_shapes=[
+            pltpu.VMEM(fine.shape, F32),
+            pltpu.VMEM((parts, layers, FIELDS, cells // parts), F32),
+            pltpu.VMEM((FIELDS, cells), F32),
+            pltpu.VMEM(skin.shape, F32),
+            pltpu.VMEM(op.shape, F32),
+            pltpu.SemaphoreType.DMA((4,)),
+            pltpu.SemaphoreType.DMA((2,)),
+            pltpu.SemaphoreType.DMA((parts,)),
+            pltpu.SemaphoreType.DMA((parts,)),
+        ],
+        compiler_params=pltpu.CompilerParams(vmem_limit_bytes=56 * 1024 * 1024),
+    )(nest, mixed, forced, heat, op)
+    return nest, jnp.transpose(marine_new, (1, 0, 2)), heat
 
 
 def solution(mesh):

time: 45.3 us -> 42.3 us (0.934)
  other arithmetic: 4.36 us -> 0 us
  Pallas kernels: 37.2 us -> 40.9 us
  local copies, waits for them, and re-layouts: 2.24 us -> 0 us
    transpose x1 -> x0, other arithmetic: 4.36 us -> none  [on_device(): jnp.transpose(marine_new, (1, 0, 2))]
    pallas_call x0 -> x1, Pallas kernels: none -> 3.18 us  [on_device(): pl.pallas_call(functools.partial(finish, parts), out_shape=(jax.ShapeDtyp...]
    unnamed x6 -> x0, local copies, waits for them, and re-layouts: 1.39 us -> none
    slice x1 -> x0, local copies, waits for them, and re-layouts: 0.85 us -> none  [on_device(): marine_new = mixed + op[:, 0][:, None, None] * forced[None]]
    pallas_call x1, Pallas kernels: 37.2 us -> 37.7 us  [on_device(): pl.pallas_call(functools.partial(kernel, nx, ny, cap, jp, rp, yw, wrows,...]
where the time goes in v5:
time: 42.3 us; the launch traced here: 42.2 us
  Pallas kernels  40.9 us (97%)
  between operations  1.29 us (3%)
    pallas_call x1, Pallas kernels, on_device(): pl.pallas_call(functools.partial(kernel, nx, ny, cap, jp, rp, yw, wrows,...  37.7 us
    pallas_call x1, Pallas kernels, on_device(): pl.pallas_call(functools.partial(finish, parts), out_shape=(jax.ShapeDtyp...  3.18 us

profile of v5, /device:TPU:0, one launch (start us, length us, event | category | flops | bytes accessed | tf_op | source)
XLA Modules:
  0.0 42.2 jit_solution(12771457322272545113)
XLA Ops:
  1.3 37.7 %shard_map.121 = (f32[4,192,96]{2,1,0:T(8,128)}, f32[41,4,4096]{2,1,0:T(4,128)}, f32[4,4096]{1,0:T(4,128)}, f32[192,96]{1,0:T(8,128)}) custom-call(s32[1]{0:T(128)S(6)} %copy.13.holder, s32[2]{0:T(128)} %corner.1, s32[1,144]{1,0:T(1,128)} %bitcast.5, s32[1,144]{1,0:T(1,128)} %bitcast.6, f32[4,192,96]{2,1,0:T(8,128)} %fine_far.1, f32[192,96]{1,0:T(8,128)} %skin_far.1, ...), custom_call_target="tpu_custom_call" | custom-call | tf_op jit(solution)/shard_map/pallas_call | solution.py:487
  39.0 3.2 %shard_map.122 = (f32[4,192,96]{2,1,0:T(8,128)}, f32[41,4,4096]{2,1,0:T(4,128)}, f32[192,96]{1,0:T(8,128)}) custom-call(f32[4,192,96]{2,1,0:T(8,128)} %get-tuple-element.10.nest, f32[41,4,4096]{2,1,0:T(4,128)} %get-tuple-element.11.mixed, f32[4,4096]{1,0:T(4,128)} %get-tuple-element.12.forced, f32[192,96]{1,0:T(8,128)} %get-tuple-element.13.heat, f32[41,41]{1,0:T(8,128)} %op.1), custom_call_target="tpu_custom_call" | custom-call | tf_op jit(solution)/shard_map/pallas_call | solution.py:545

commit v6 on v5

--- a/solution.py
+++ b/solution.py
@@ -83,7 +83,7 @@
             return
 
         def nth(n):
-            return me ^ (((n & 1) << 2) | ((n >> 1) & 3) | ((n >> 3) << 3))
+            return (me + n) & (devices - 1)
 
         each(devices - 1, lambda n: work(nth(n + 1)))
 
@@ -345,7 +345,7 @@
 
     def dispatch(c):
         if power:
-            turn = ((c + 1) & (turns - 1)) ^ (me >> (per.bit_length() - 1))
+            turn = (c + 1 + (me >> (per.bit_length() - 1))) & (turns - 1)
         else:
             turn = lax.rem(c + lax.div(me, per), turns)
         rows = pl.ds(pl.multiple_of(turn * chunk, chunk), chunk)

time: 42.3 us -> 41.3 us (0.976)
  Pallas kernels: 40.9 us -> 39.8 us
    pallas_call x1, Pallas kernels: 37.7 us -> 36.6 us  [on_device(): pl.pallas_call(functools.partial(kernel, nx, ny, cap, jp, rp, yw, wrows,...]
where the time goes in v6:
time: 41.3 us; the launch traced here: 41.1 us
  Pallas kernels  39.8 us (96%)
  between operations  1.29 us (3%)
    pallas_call x1, Pallas kernels, on_device(): pl.pallas_call(functools.partial(kernel, nx, ny, cap, jp, rp, yw, wrows,...  36.6 us
    pallas_call x1, Pallas kernels, on_device(): pl.pallas_call(functools.partial(finish, parts), out_shape=(jax.ShapeDtyp...  3.18 us

profile of v6, /device:TPU:0, one launch (start us, length us, event | category | flops | bytes accessed | tf_op | source)
XLA Modules:
  0.0 41.1 jit_solution(13340801831400611892)
XLA Ops:
  1.3 36.6 %shard_map.121 = (f32[4,192,96]{2,1,0:T(8,128)}, f32[41,4,4096]{2,1,0:T(4,128)}, f32[4,4096]{1,0:T(4,128)}, f32[192,96]{1,0:T(8,128)}) custom-call(s32[1]{0:T(128)S(6)} %copy.13.holder, s32[2]{0:T(128)} %corner.1, s32[1,144]{1,0:T(1,128)} %bitcast.5, s32[1,144]{1,0:T(1,128)} %bitcast.6, f32[4,192,96]{2,1,0:T(8,128)} %fine_far.1, f32[192,96]{1,0:T(8,128)} %skin_far.1, ...), custom_call_target="tpu_custom_call" | custom-call | tf_op jit(solution)/shard_map/pallas_call | solution.py:487
  37.9 3.2 %shard_map.122 = (f32[4,192,96]{2,1,0:T(8,128)}, f32[41,4,4096]{2,1,0:T(4,128)}, f32[192,96]{1,0:T(8,128)}) custom-call(f32[4,192,96]{2,1,0:T(8,128)} %get-tuple-element.10.nest, f32[41,4,4096]{2,1,0:T(4,128)} %get-tuple-element.11.mixed, f32[4,4096]{1,0:T(4,128)} %get-tuple-element.12.forced, f32[192,96]{1,0:T(8,128)} %get-tuple-element.13.heat, f32[41,41]{1,0:T(8,128)} %op.1), custom_call_target="tpu_custom_call" | custom-call | tf_op jit(solution)/shard_map/pallas_call | solution.py:545
